TPU v7x, 32 devices: a whole 2x2x4 slice. The times are simulated.
32 devices in a mesh: cuts: 2 (over x), brick: 16 (over z, y, core).
Axes of the slice: x: 2, y: 2, z: 4, core: 2. Of those that a mesh axis runs over, the one named last changes fastest.
Arguments:
- eigen_vectors: float32 [64, 2, 3, 64, 512], P(None, None, None, ('cuts', 'brick')), parts along dimension 3, may hold values from -6 to 6
- link_field: float32 [3, 2, 3, 3, 64, 512], P(None, None, None, None, ('cuts', 'brick')), parts along dimension 4, may hold values from -3 to 3
- block_slot: int32 [63], replicated, may hold values from 0 to 63, as said below
Outputs:
- elementals: float32 [128, 32, 128], P(('cuts', 'brick')), parts along dimension 0
There are 2 independent parts, one for each index of `cuts`. A program takes and returns all parts, laid end to end along the dimension named above; an argument that names none is the same for every part. Nothing has to cross between parts.
Inputs may be any that keep to these rules, and one draw needn't show every extreme that they name: block_slot names distinct slots; slot s belongs to device s // 4 of the brick axis; in every draw some device has all 4 of its slots named.
All inputs are finite; a program needn't handle non-finite values.
Results may differ from a plain program's by a relative error of at most 0.0044.
Values sent between devices are 32-bit elements; how exact they have to be, the bound alone decides.
No kernel may reach another device: no remote copies, remote signals or barrier semaphores. Data moves between devices by JAX's collectives and lax.ppermute only.
A program may use at most 64 MiB of HBM per device.

v0:
```python
import math

import jax
import jax.numpy as jnp
import numpy as np
from jax import lax
from jax.sharding import PartitionSpec as P

PB = 32
CAP = 4
LX = 8
LY = 64


def padded(cells, sides, width):
    for axis, dim in sides:
        count = lax.axis_size(axis)
        head = lax.slice_in_dim(cells, 0, width, axis=dim)
        tail = lax.slice_in_dim(cells, cells.shape[dim] - width, cells.shape[dim], axis=dim)
        cells = jnp.concatenate(
            [
                lax.ppermute(tail, axis, [(i, (i + 1) % count) for i in range(count)]),
                cells,
                lax.ppermute(head, axis, [((i + 1) % count, i) for i in range(count)]),
            ],
            axis=dim,
        )
    return cells


def from_behind(block, axis, distance):
    devices = range(lax.axis_size(axis))
    route = [((i - distance) % len(devices), i) for i in devices]
    return lax.ppermute(block, axis, route)


def shift_columns(lattice_field, forward):
    column = jnp.arange(lattice_field.shape[-1]) % LX
    if forward:
        return jnp.where(
            column == LX - 1,
            jnp.roll(lattice_field, LX - 1, axis=-1),
            jnp.roll(lattice_field, -1, axis=-1),
        )
    return jnp.where(
        column == 0,
        jnp.roll(lattice_field, -(LX - 1), axis=-1),
        jnp.roll(lattice_field, 1, axis=-1),
    )


def link_times(link_set, lattice_field):
    real_rows = []
    imag_rows = []
    for out_row in range(3):
        real_part = (
            link_set[0, out_row, 0] * lattice_field[:, 0, 0]
            - link_set[1, out_row, 0] * lattice_field[:, 1, 0]
        )
        imag_part = (
            link_set[0, out_row, 0] * lattice_field[:, 1, 0]
            + link_set[1, out_row, 0] * lattice_field[:, 0, 0]
        )
        for in_row in (1, 2):
            real_part = (
                real_part
                + link_set[0, out_row, in_row] * lattice_field[:, 0, in_row]
                - link_set[1, out_row, in_row] * lattice_field[:, 1, in_row]
            )
            imag_part = (
                imag_part
                + link_set[0, out_row, in_row] * lattice_field[:, 1, in_row]
                + link_set[1, out_row, in_row] * lattice_field[:, 0, in_row]
            )
        real_rows.append(real_part)
        imag_rows.append(imag_part)
    return jnp.stack([jnp.stack(real_rows, 1), jnp.stack(imag_rows, 1)], 1)


def adjoint_times(link_set, lattice_field):
    real_rows = []
    imag_rows = []
    for out_row in range(3):
        real_part = (
            link_set[0, 0, out_row] * lattice_field[:, 0, 0]
            + link_set[1, 0, out_row] * lattice_field[:, 1, 0]
        )
        imag_part = (
            link_set[0, 0, out_row] * lattice_field[:, 1, 0]
            - link_set[1, 0, out_row] * lattice_field[:, 0, 0]
        )
        for in_row in (1, 2):
            real_part = (
                real_part
                + link_set[0, in_row, out_row] * lattice_field[:, 0, in_row]
                + link_set[1, in_row, out_row] * lattice_field[:, 1, in_row]
            )
            imag_part = (
                imag_part
                + link_set[0, in_row, out_row] * lattice_field[:, 1, in_row]
                - link_set[1, in_row, out_row] * lattice_field[:, 0, in_row]
            )
        real_rows.append(real_part)
        imag_rows.append(imag_part)
    return jnp.stack([jnp.stack(real_rows, 1), jnp.stack(imag_rows, 1)], 1)


def apply_hops(lattice_field, link_field):
    inner_field = lattice_field[:, :, :, 1:-1]
    inner_links = link_field[:, :, :, :, 1:-1]
    hop_total = link_times(inner_links[0], shift_columns(inner_field, True))
    hop_total = hop_total + shift_columns(adjoint_times(inner_links[0], inner_field), False)
    hop_total = hop_total + link_times(inner_links[1], jnp.roll(inner_field, -LX, axis=4))
    hop_total = hop_total + jnp.roll(adjoint_times(inner_links[1], inner_field), LX, axis=4)
    hop_total = hop_total + link_times(link_field[2][:, :, :, 1:-1], lattice_field[:, :, :, 2:])
    hop_total = hop_total + adjoint_times(link_field[2][:, :, :, :-2], lattice_field[:, :, :, :-2])
    return hop_total * (1.0 / 6.0)


def diquark_grid(left_rows, right_rows):
    left = left_rows[:, None]
    right = right_rows[None]
    real_rows = []
    imag_rows = []
    for colour in range(3):
        first_colour = (colour + 1) % 3
        second_colour = (colour + 2) % 3
        real_part = (
            left[:, :, 0, first_colour] * right[:, :, 0, second_colour]
            - left[:, :, 1, first_colour] * right[:, :, 1, second_colour]
            - (
                left[:, :, 0, second_colour] * right[:, :, 0, first_colour]
                - left[:, :, 1, second_colour] * right[:, :, 1, first_colour]
            )
        )
        imag_part = (
            left[:, :, 0, first_colour] * right[:, :, 1, second_colour]
            + left[:, :, 1, first_colour] * right[:, :, 0, second_colour]
            - (
                left[:, :, 0, second_colour] * right[:, :, 1, first_colour]
                + left[:, :, 1, second_colour] * right[:, :, 0, first_colour]
            )
        )
        real_rows.append(real_part)
        imag_rows.append(imag_part)
    return jnp.stack([jnp.stack(real_rows, 2), jnp.stack(imag_rows, 2)], 2)


def elemental_block(quarks, vectors_low):
    pair_count = quarks.shape[0]
    vector_count = vectors_low.shape[0]
    left_mat = quarks.reshape(pair_count * 2, -1)
    right_mat = vectors_low.reshape(vector_count * 2, -1)
    products = lax.dot_general(
        left_mat, right_mat, (((1,), (1,)), ((), ())), preferred_element_type=jnp.float32
    )
    products = products.reshape(pair_count, 2, vector_count, 2)
    real_part = products[:, 0, :, 0] - products[:, 1, :, 1]
    imag_part = products[:, 0, :, 1] + products[:, 1, :, 0]
    return jnp.stack([real_part, imag_part], 1).reshape(pair_count, 2 * vector_count)


def grow_rim(lattice_field):
    return padded(lattice_field, (("brick", 3),), 1)


def on_device(eigen_vectors, link_field, block_slot):
    rim_depth = 1
    plane_total = link_field.shape[4]
    lower_links = from_behind(link_field[:, :, :, :, plane_total - rim_depth :], "brick", 1)
    unused_plane = jnp.zeros_like(link_field[:, :, :, :, :1])
    link_wide = jnp.concatenate([lower_links, link_field, unused_plane], 4)
    first_step = apply_hops(grow_rim(eigen_vectors), link_wide)
    filtered = 2.0 * apply_hops(grow_rim(first_step), link_wide) - eigen_vectors
    vectors_low = filtered.astype(jnp.bfloat16)
    vector_count = filtered.shape[0]
    group_width = 8
    group_count = vector_count // group_width
    left_groups = filtered.reshape((group_count, group_width) + filtered.shape[1:])

    def one_group(left_rows):
        quarks = diquark_grid(left_rows, filtered).astype(jnp.bfloat16)
        quarks = quarks.reshape((group_width * vector_count,) + quarks.shape[2:])
        return elemental_block(quarks, vectors_low)

    grid_sums = lax.map(one_group, left_groups).reshape(
        vector_count * vector_count, 2 * vector_count
    )
    first_index, second_index = np.triu_indices(vector_count, 1)
    pair_rows = jnp.asarray((first_index * vector_count + second_index).astype(np.int32))
    block_count = first_index.shape[0] // PB
    partial_value = jnp.take(grid_sums, pair_rows, axis=0)
    brick_count = lax.axis_size("brick")
    lattice_depth = filtered.shape[3] * brick_count
    factor = 1.0 / math.sqrt(3.0 * LX * LY * lattice_depth)
    partial_value = partial_value.reshape(block_count, PB, 2 * vector_count) * factor
    slot_total = CAP * brick_count
    placed = (
        jnp.zeros((slot_total, PB, 2 * vector_count), jnp.float32).at[block_slot].set(partial_value)
    )
    return lax.psum_scatter(placed, "brick", scatter_dimension=0, tiled=True)


def solution(mesh):
    return jax.shard_map(
        on_device,
        mesh=mesh,
        in_specs=(
            P(None, None, None, ("cuts", "brick"), None),
            P(None, None, None, None, ("cuts", "brick"), None),
            P(),
        ),
        out_specs=P(("cuts", "brick"), None, None),
        check_vma=False,
    )
```

profile of v0, /device:TPU:0, one launch (start us, length us, event | category | flops | bytes accessed | tf_op | source)
XLA Modules:
  0.0 500.2 jit_solution(3694763689882053251)
XLA Ops:
  6.5 1.7 slice.528
  8.7 1.9 copy.24
  10.6 1.3 fusion.77
  11.9 2.6 collective-permute-start.2
  14.5 2.4 collective-permute-start.1
  27.7 1.2 multiply_subtract_fusion.28
  30.9 1.3 pad_clamp_fusion
  32.2 1.2 compare_select_fusion
  33.5 1.6 maximum_bitcast_fusion.6
  38.5 1.2 constant_dynamic-update-slice_fusion.4
  41.0 1.2 constant_dynamic-update-slice_fusion.1
  43.9 1.9 fusion.20
  54.6 8.0 %collective-permute-done.3 = f32[64,2,3,1,512]{4,0,3,2,1:T(8,128)S(1)} collective-permute-done((f32[64,2,3,1,512]{4,0,3,2,1:T(8,128)S(1)}, f32[64,2,3,1,512]{4,0,3,2,1:T(8,128)S(1)}, u32[]{:S(2)}, u32[]{:S(2)}) %collective-permute-start.3) | collective-permute-done | bytes 786464 | tf_op jit(solution)/shard_map/ppermute | solution.py:24
  63.4 4.0 collective-permute-done.4
  68.4 3.3 fusion.60
  71.8 2.6 copy.42
  75.2 1.5 reshape.5706
  76.7 343.0 %while.11 = (s32[]{:T(128)}, f32[8,512,128]{2,1,0:T(8,128)}, f32[8,8,2,3,2,512]{5,1,0,4,3,2:T(8,128)}, f32[64,2,3,2,512]{4,3,0,2,1:T(2,128)S(1)}, bf16[64,2,3,2,...) while((s32[]{:T(128)}, f32[8,512,128]{2,1,0:T(8,128)}, ...), condition=%wide.wide.region_1.2_spmd, body=%wide.wide.region_0.1_spmd.sunk | while | flops 849477632 | bytes 60097160 | solution.py:186
  76.7 1.2 constant_dynamic-slice_fusion.3
  78.7 13.5 %subtract_convert_fusion.8 = (bf16[8,64,1,2,512]{4,3,2,1,0:T(2,128)(2,1)S(1)}, bf16[8,64,1,2,512]{4,3,2,1,0:T(2,128)(2,1)S(1)}, bf16[8,64,1,2,512]{4,3,2,1,0:T(2...) fusion(f32[64,2,512]{2,1,0:T(2,128)S(1)} %get-tuple-element.365, ...), kind=kLoop, calls=%fused_computation.11.clone.clone.1 | loop fusion | flops 25165824 | bytes 8060928 | tf_op jit(solution)/shard_map/convert.7
  92.2 9.7 %pad_maximum_fusion.18 = (bf16[8,64,3,2,512]{4,3,2,1,0:T(2,128)(2,1)S(1)}, bf16[8,64,3,2,512]{4,3,2,1,0:T(2,128)(2,1)}) fusion(bf16[8,64,1,2,512]{4,3,2,1,0:T(2,128)(2,1)S(1)} %get-tuple-element.377, bf16[8,64,1,2,512]{4,3,2,1,0:T(2,128)(2,1)S(1)} %get-tuple-element.378, bf16[8,64,1,2,512]{4,3,2,1,0:T(2,128)(2,1)S(1)} %get-tuple-element.379, ...), kind=kLoop, calls=%fused_computation.4.clone.clone.1 | loop fusion | flops 6291456 | bytes 12582912 | tf_op jit(solution)/shard_map/while/body/eval_jaxpr/stack | solution.py:146
  101.9 8.2 %stack.344 = bf16[512,1,3072]{2,0,1:T(8,128)(2,1)} reshape(bf16[8,64,3,2,512]{4,3,2,1,0:T(2,128)(2,1)} %get-tuple-element.383) | data formatting | bytes 6291456 | tf_op jit(solution)/shard_map/while/body/eval_jaxpr/stack | solution.py:146
  110.1 3.6 stack.345
  113.7 4.5 fusion.86
  119.7 1.1 constant_dynamic-slice_fusion.3
  121.5 13.5 %subtract_convert_fusion.8 = (bf16[8,64,1,2,512]{4,3,2,1,0:T(2,128)(2,1)S(1)}, bf16[8,64,1,2,512]{4,3,2,1,0:T(2,128)(2,1)S(1)}, bf16[8,64,1,2,512]{4,3,2,1,0:T(2...) fusion(f32[64,2,512]{2,1,0:T(2,128)S(1)} %get-tuple-element.365, ...), kind=kLoop, calls=%fused_computation.11.clone.clone.1 | loop fusion | flops 25165824 | bytes 8060928 | tf_op jit(solution)/shard_map/convert.7
  135.0 9.7 %pad_maximum_fusion.18 = (bf16[8,64,3,2,512]{4,3,2,1,0:T(2,128)(2,1)S(1)}, bf16[8,64,3,2,512]{4,3,2,1,0:T(2,128)(2,1)}) fusion(bf16[8,64,1,2,512]{4,3,2,1,0:T(2,128)(2,1)S(1)} %get-tuple-element.377, bf16[8,64,1,2,512]{4,3,2,1,0:T(2,128)(2,1)S(1)} %get-tuple-element.378, bf16[8,64,1,2,512]{4,3,2,1,0:T(2,128)(2,1)S(1)} %get-tuple-element.379, ...), kind=kLoop, calls=%fused_computation.4.clone.clone.1 | loop fusion | flops 6291456 | bytes 12582912 | tf_op jit(solution)/shard_map/while/body/eval_jaxpr/stack | solution.py:146
  144.7 8.2 %stack.344 = bf16[512,1,3072]{2,0,1:T(8,128)(2,1)} reshape(bf16[8,64,3,2,512]{4,3,2,1,0:T(2,128)(2,1)} %get-tuple-element.383) | data formatting | bytes 6291456 | tf_op jit(solution)/shard_map/while/body/eval_jaxpr/stack | solution.py:146
  152.9 3.6 stack.345
  156.5 4.5 fusion.86
  162.5 1.1 constant_dynamic-slice_fusion.3
  164.4 13.5 %subtract_convert_fusion.8 = (bf16[8,64,1,2,512]{4,3,2,1,0:T(2,128)(2,1)S(1)}, bf16[8,64,1,2,512]{4,3,2,1,0:T(2,128)(2,1)S(1)}, bf16[8,64,1,2,512]{4,3,2,1,0:T(2...) fusion(f32[64,2,512]{2,1,0:T(2,128)S(1)} %get-tuple-element.365, ...), kind=kLoop, calls=%fused_computation.11.clone.clone.1 | loop fusion | flops 25165824 | bytes 8060928 | tf_op jit(solution)/shard_map/convert.7
  177.9 9.7 %pad_maximum_fusion.18 = (bf16[8,64,3,2,512]{4,3,2,1,0:T(2,128)(2,1)S(1)}, bf16[8,64,3,2,512]{4,3,2,1,0:T(2,128)(2,1)}) fusion(bf16[8,64,1,2,512]{4,3,2,1,0:T(2,128)(2,1)S(1)} %get-tuple-element.377, bf16[8,64,1,2,512]{4,3,2,1,0:T(2,128)(2,1)S(1)} %get-tuple-element.378, bf16[8,64,1,2,512]{4,3,2,1,0:T(2,128)(2,1)S(1)} %get-tuple-element.379, ...), kind=kLoop, calls=%fused_computation.4.clone.clone.1 | loop fusion | flops 6291456 | bytes 12582912 | tf_op jit(solution)/shard_map/while/body/eval_jaxpr/stack | solution.py:146
  187.6 8.2 %stack.344 = bf16[512,1,3072]{2,0,1:T(8,128)(2,1)} reshape(bf16[8,64,3,2,512]{4,3,2,1,0:T(2,128)(2,1)} %get-tuple-element.383) | data formatting | bytes 6291456 | tf_op jit(solution)/shard_map/while/body/eval_jaxpr/stack | solution.py:146
  195.8 3.6 stack.345
  199.4 4.5 fusion.86
  207.3 13.5 %subtract_convert_fusion.8 = (bf16[8,64,1,2,512]{4,3,2,1,0:T(2,128)(2,1)S(1)}, bf16[8,64,1,2,512]{4,3,2,1,0:T(2,128)(2,1)S(1)}, bf16[8,64,1,2,512]{4,3,2,1,0:T(2...) fusion(f32[64,2,512]{2,1,0:T(2,128)S(1)} %get-tuple-element.365, ...), kind=kLoop, calls=%fused_computation.11.clone.clone.1 | loop fusion | flops 25165824 | bytes 8060928 | tf_op jit(solution)/shard_map/convert.7
  220.8 9.7 %pad_maximum_fusion.18 = (bf16[8,64,3,2,512]{4,3,2,1,0:T(2,128)(2,1)S(1)}, bf16[8,64,3,2,512]{4,3,2,1,0:T(2,128)(2,1)}) fusion(bf16[8,64,1,2,512]{4,3,2,1,0:T(2,128)(2,1)S(1)} %get-tuple-element.377, bf16[8,64,1,2,512]{4,3,2,1,0:T(2,128)(2,1)S(1)} %get-tuple-element.378, bf16[8,64,1,2,512]{4,3,2,1,0:T(2,128)(2,1)S(1)} %get-tuple-element.379, ...), kind=kLoop, calls=%fused_computation.4.clone.clone.1 | loop fusion | flops 6291456 | bytes 12582912 | tf_op jit(solution)/shard_map/while/body/eval_jaxpr/stack | solution.py:146
  230.5 8.2 %stack.344 = bf16[512,1,3072]{2,0,1:T(8,128)(2,1)} reshape(bf16[8,64,3,2,512]{4,3,2,1,0:T(2,128)(2,1)} %get-tuple-element.383) | data formatting | bytes 6291456 | tf_op jit(solution)/shard_map/while/body/eval_jaxpr/stack | solution.py:146
  238.7 3.6 stack.345
  242.3 4.5 fusion.86
  250.1 13.5 %subtract_convert_fusion.8 = (bf16[8,64,1,2,512]{4,3,2,1,0:T(2,128)(2,1)S(1)}, bf16[8,64,1,2,512]{4,3,2,1,0:T(2,128)(2,1)S(1)}, bf16[8,64,1,2,512]{4,3,2,1,0:T(2...) fusion(f32[64,2,512]{2,1,0:T(2,128)S(1)} %get-tuple-element.365, ...), kind=kLoop, calls=%fused_computation.11.clone.clone.1 | loop fusion | flops 25165824 | bytes 8060928 | tf_op jit(solution)/shard_map/convert.7
  263.6 9.7 %pad_maximum_fusion.18 = (bf16[8,64,3,2,512]{4,3,2,1,0:T(2,128)(2,1)S(1)}, bf16[8,64,3,2,512]{4,3,2,1,0:T(2,128)(2,1)}) fusion(bf16[8,64,1,2,512]{4,3,2,1,0:T(2,128)(2,1)S(1)} %get-tuple-element.377, bf16[8,64,1,2,512]{4,3,2,1,0:T(2,128)(2,1)S(1)} %get-tuple-element.378, bf16[8,64,1,2,512]{4,3,2,1,0:T(2,128)(2,1)S(1)} %get-tuple-element.379, ...), kind=kLoop, calls=%fused_computation.4.clone.clone.1 | loop fusion | flops 6291456 | bytes 12582912 | tf_op jit(solution)/shard_map/while/body/eval_jaxpr/stack | solution.py:146
  273.3 8.2 %stack.344 = bf16[512,1,3072]{2,0,1:T(8,128)(2,1)} reshape(bf16[8,64,3,2,512]{4,3,2,1,0:T(2,128)(2,1)} %get-tuple-element.383) | data formatting | bytes 6291456 | tf_op jit(solution)/shard_map/while/body/eval_jaxpr/stack | solution.py:146
  281.5 3.6 stack.345
  285.1 4.5 fusion.86
  293.0 13.5 %subtract_convert_fusion.8 = (bf16[8,64,1,2,512]{4,3,2,1,0:T(2,128)(2,1)S(1)}, bf16[8,64,1,2,512]{4,3,2,1,0:T(2,128)(2,1)S(1)}, bf16[8,64,1,2,512]{4,3,2,1,0:T(2...) fusion(f32[64,2,512]{2,1,0:T(2,128)S(1)} %get-tuple-element.365, ...), kind=kLoop, calls=%fused_computation.11.clone.clone.1 | loop fusion | flops 25165824 | bytes 8060928 | tf_op jit(solution)/shard_map/convert.7
  306.5 9.7 %pad_maximum_fusion.18 = (bf16[8,64,3,2,512]{4,3,2,1,0:T(2,128)(2,1)S(1)}, bf16[8,64,3,2,512]{4,3,2,1,0:T(2,128)(2,1)}) fusion(bf16[8,64,1,2,512]{4,3,2,1,0:T(2,128)(2,1)S(1)} %get-tuple-element.377, bf16[8,64,1,2,512]{4,3,2,1,0:T(2,128)(2,1)S(1)} %get-tuple-element.378, bf16[8,64,1,2,512]{4,3,2,1,0:T(2,128)(2,1)S(1)} %get-tuple-element.379, ...), kind=kLoop, calls=%fused_computation.4.clone.clone.1 | loop fusion | flops 6291456 | bytes 12582912 | tf_op jit(solution)/shard_map/while/body/eval_jaxpr/stack | solution.py:146
  316.2 8.2 %stack.344 = bf16[512,1,3072]{2,0,1:T(8,128)(2,1)} reshape(bf16[8,64,3,2,512]{4,3,2,1,0:T(2,128)(2,1)} %get-tuple-element.383) | data formatting | bytes 6291456 | tf_op jit(solution)/shard_map/while/body/eval_jaxpr/stack | solution.py:146
  324.4 3.6 stack.345
  328.0 4.5 fusion.86
  335.9 13.5 %subtract_convert_fusion.8 = (bf16[8,64,1,2,512]{4,3,2,1,0:T(2,128)(2,1)S(1)}, bf16[8,64,1,2,512]{4,3,2,1,0:T(2,128)(2,1)S(1)}, bf16[8,64,1,2,512]{4,3,2,1,0:T(2...) fusion(f32[64,2,512]{2,1,0:T(2,128)S(1)} %get-tuple-element.365, ...), kind=kLoop, calls=%fused_computation.11.clone.clone.1 | loop fusion | flops 25165824 | bytes 8060928 | tf_op jit(solution)/shard_map/convert.7
  349.4 9.7 %pad_maximum_fusion.18 = (bf16[8,64,3,2,512]{4,3,2,1,0:T(2,128)(2,1)S(1)}, bf16[8,64,3,2,512]{4,3,2,1,0:T(2,128)(2,1)}) fusion(bf16[8,64,1,2,512]{4,3,2,1,0:T(2,128)(2,1)S(1)} %get-tuple-element.377, bf16[8,64,1,2,512]{4,3,2,1,0:T(2,128)(2,1)S(1)} %get-tuple-element.378, bf16[8,64,1,2,512]{4,3,2,1,0:T(2,128)(2,1)S(1)} %get-tuple-element.379, ...), kind=kLoop, calls=%fused_computation.4.clone.clone.1 | loop fusion | flops 6291456 | bytes 12582912 | tf_op jit(solution)/shard_map/while/body/eval_jaxpr/stack | solution.py:146
  359.1 8.2 %stack.344 = bf16[512,1,3072]{2,0,1:T(8,128)(2,1)} reshape(bf16[8,64,3,2,512]{4,3,2,1,0:T(2,128)(2,1)} %get-tuple-element.383) | data formatting | bytes 6291456 | tf_op jit(solution)/shard_map/while/body/eval_jaxpr/stack | solution.py:146
  367.3 3.6 stack.345
  370.9 4.5 fusion.86
  378.8 13.5 %subtract_convert_fusion.8 = (bf16[8,64,1,2,512]{4,3,2,1,0:T(2,128)(2,1)S(1)}, bf16[8,64,1,2,512]{4,3,2,1,0:T(2,128)(2,1)S(1)}, bf16[8,64,1,2,512]{4,3,2,1,0:T(2...) fusion(f32[64,2,512]{2,1,0:T(2,128)S(1)} %get-tuple-element.365, ...), kind=kLoop, calls=%fused_computation.11.clone.clone.1 | loop fusion | flops 25165824 | bytes 8060928 | tf_op jit(solution)/shard_map/convert.7
  392.3 9.7 %pad_maximum_fusion.18 = (bf16[8,64,3,2,512]{4,3,2,1,0:T(2,128)(2,1)S(1)}, bf16[8,64,3,2,512]{4,3,2,1,0:T(2,128)(2,1)}) fusion(bf16[8,64,1,2,512]{4,3,2,1,0:T(2,128)(2,1)S(1)} %get-tuple-element.377, bf16[8,64,1,2,512]{4,3,2,1,0:T(2,128)(2,1)S(1)} %get-tuple-element.378, bf16[8,64,1,2,512]{4,3,2,1,0:T(2,128)(2,1)S(1)} %get-tuple-element.379, ...), kind=kLoop, calls=%fused_computation.4.clone.clone.1 | loop fusion | flops 6291456 | bytes 12582912 | tf_op jit(solution)/shard_map/while/body/eval_jaxpr/stack | solution.py:146
  402.0 8.2 %stack.344 = bf16[512,1,3072]{2,0,1:T(8,128)(2,1)} reshape(bf16[8,64,3,2,512]{4,3,2,1,0:T(2,128)(2,1)} %get-tuple-element.383) | data formatting | bytes 6291456 | tf_op jit(solution)/shard_map/while/body/eval_jaxpr/stack | solution.py:146
  410.2 3.6 stack.345
  413.8 4.5 fusion.86
  419.8 7.2 %gather_fusion = f32[2016,128]{1,0:T(8,128)S(1)} fusion(f32[4096,128]{1,0:T(8,128)} %bitcast.992, s32[2048]{0:T(1024)S(1)} %copy-done.84), kind=kCustom, calls=%fused_computation | custom fusion | bytes 2072448 | tf_op jit(solution)/shard_map/jit(_take)/gather | solution.py:192
  427.5 2.8 scatter_fusion
  431.4 62.0 %reduce-scatter.2.cloned.1.call-done = f32[4,32,128]{2,1,0:T(8,128)} async-done(((f32[64,32,128]{2,1,0:T(8,128)}), f32[4,32,128]{2,1,0:T(8,128)}) %reduce-scatter.2.cloned.1.call-update) | async-done | bytes 65552 | tf_op jit(solution)/shard_map/reduce_scatter | solution.py:201
  (358 shorter events, 55.0 us)
Async XLA Ops:
  6.5 486.8 %reduce-scatter.2.cloned.1.call-start = ((), (), s32[]{:S(2)}) async-start(), calls=%async_computation.1 | async-start | bytes 1114112 | tf_op jit(solution)/shard_map/reduce_scatter | solution.py:201
  8.2 28.5 %collective-permute-start = (f32[3,2,3,3,1,512]{5,4,3,2,1,0:T(1,128)}, f32[3,2,3,3,1,512]{5,4,3,2,1,0:T(1,128)}, u32[]{:S(2)}, u32[]{:S(2)}) collective-permute-start(f32[3,2,3,3,1,512]{5,4,3,2,1,0:T(1,128)} %slice.528), channel_id=1, source_target_pairs={{15,0},{0,1},{1,2},{2,3},{3,4},{4,5},{5,6},{6,7},{7,8},{8,9},{9,10... | collective-permute-start | bytes 331784 | tf_op jit(solution)/shard_map/ppermute | solution.py:34
  10.6 6.3 %copy-start.18 = (f32[3,2,3,3,2,512]{5,4,3,2,1,0:T(2,128)S(1)}, f32[3,2,3,3,2,512]{5,4,3,2,1,0:T(2,128)}, u32[]{:S(2)}) copy-start(f32[3,2,3,3,2,512]{5,4,3,2,1,0:T(2,128)} %param.7) | copy-start | bytes 663556
  11.9 26.7 %collective-permute-start.2 = (f32[64,2,3,1,512]{4,0,3,2,1:T(8,128)}, f32[64,2,3,1,512]{4,0,3,2,1:T(8,128)}, u32[]{:S(2)}, u32[]{:S(2)}) collective-permute-start(f32[64,2,3,1,512]{4,0,3,2,1:T(8,128)} %get-tuple-element.175), channel_id=1, source_target_pairs={{0,1},{1,2},{2,3},{3,4},{4,5},{5,6},{6,7},{7,8},{8,9},{9,10},{10,1... | collective-permute-start | bytes 2359304 | tf_op jit(solution)/shard_map/ppermute | solution.py:22
  14.5 26.5 %collective-permute-start.1 = (f32[64,2,3,1,512]{4,0,3,2,1:T(8,128)}, f32[64,2,3,1,512]{4,0,3,2,1:T(8,128)}, u32[]{:S(2)}, u32[]{:S(2)}) collective-permute-start(f32[64,2,3,1,512]{4,0,3,2,1:T(8,128)} %get-tuple-element.176), channel_id=1, source_target_pairs={{1,0},{2,1},{3,2},{4,3},{5,4},{6,5},{7,6},{8,7},{9,8},{10,9},{11,1... | collective-permute-start | bytes 2359304 | tf_op jit(solution)/shard_map/ppermute | solution.py:24
  17.4 3.8 copy-start.40
  17.4 3.8 copy-start.42
  17.4 3.8 copy-start.52
  17.4 3.8 copy-start.54
  17.5 3.8 copy-start.56
  17.5 3.8 copy-start.66
  17.5 4.8 copy-start.36
  17.5 4.8 copy-start.38
  17.5 4.8 copy-start.48
  17.5 4.8 copy-start.50
  17.5 4.8 copy-start.62
  17.5 4.8 copy-start.64
  17.5 5.8 %copy-start.32 = (f32[2,512]{1,0:T(2,128)}, f32[2,512]{1,0:T(2,128)S(1)}, u32[]{:S(2)}) copy-start(f32[2,512]{1,0:T(2,128)S(1)} %get-tuple-element.217) | copy-start | bytes 12292
  17.5 5.8 %copy-start.34 = (f32[2,512]{1,0:T(2,128)}, f32[2,512]{1,0:T(2,128)S(1)}, u32[]{:S(2)}) copy-start(f32[2,512]{1,0:T(2,128)S(1)} %get-tuple-element.218) | copy-start | bytes 12292
  17.6 5.8 %copy-start.44 = (f32[2,512]{1,0:T(2,128)}, f32[2,512]{1,0:T(2,128)S(1)}, u32[]{:S(2)}) copy-start(f32[2,512]{1,0:T(2,128)S(1)} %get-tuple-element.219) | copy-start | bytes 12292
  17.6 5.8 %copy-start.46 = (f32[2,512]{1,0:T(2,128)}, f32[2,512]{1,0:T(2,128)S(1)}, u32[]{:S(2)}) copy-start(f32[2,512]{1,0:T(2,128)S(1)} %get-tuple-element.220) | copy-start | bytes 12292
  17.6 5.8 %copy-start.58 = (f32[2,512]{1,0:T(2,128)}, f32[2,512]{1,0:T(2,128)S(1)}, u32[]{:S(2)}) copy-start(f32[2,512]{1,0:T(2,128)S(1)} %get-tuple-element.221) | copy-start | bytes 12292
  17.6 5.8 %copy-start.60 = (f32[2,512]{1,0:T(2,128)}, f32[2,512]{1,0:T(2,128)S(1)}, u32[]{:S(2)}) copy-start(f32[2,512]{1,0:T(2,128)S(1)} %get-tuple-element.222) | copy-start | bytes 12292
  24.4 3.3 copy-start.20
  24.4 3.3 copy-start.22
  24.4 3.3 copy-start.72
  24.4 3.3 copy-start.74
  24.4 3.3 copy-start.80
  24.4 3.3 copy-start.82
  24.4 4.5 copy-start.68
  24.4 4.4 copy-start.70
  24.4 4.4 copy-start.76
  24.4 4.4 copy-start.78
  24.5 5.4 %copy-start.24 = (f32[2,512]{1,0:T(2,128)}, f32[2,512]{1,0:T(2,128)S(1)}, u32[]{:S(2)}) copy-start(f32[2,512]{1,0:T(2,128)S(1)} %get-tuple-element.235) | copy-start | bytes 12292
  24.5 5.4 %copy-start.26 = (f32[2,512]{1,0:T(2,128)}, f32[2,512]{1,0:T(2,128)S(1)}, u32[]{:S(2)}) copy-start(f32[2,512]{1,0:T(2,128)S(1)} %get-tuple-element.236) | copy-start | bytes 12292
  24.5 5.4 %copy-start.28 = (f32[2,512]{1,0:T(2,128)}, f32[2,512]{1,0:T(2,128)S(1)}, u32[]{:S(2)}) copy-start(f32[2,512]{1,0:T(2,128)S(1)} %get-tuple-element.241) | copy-start | bytes 12292
  24.5 5.4 %copy-start.30 = (f32[2,512]{1,0:T(2,128)}, f32[2,512]{1,0:T(2,128)S(1)}, u32[]{:S(2)}) copy-start(f32[2,512]{1,0:T(2,128)S(1)} %get-tuple-element.242) | copy-start | bytes 12292
  33.5 1.7 copy-start.6
  33.5 1.7 copy-start.7
  33.5 1.7 copy-start.8
  33.5 1.7 copy-start.9
  33.5 1.7 copy-start.10
  33.5 1.8 copy-start.11
  36.7 3.0 copy-start.2
  52.4 10.2 %collective-permute-start.3 = (f32[64,2,3,1,512]{4,0,3,2,1:T(8,128)S(1)}, f32[64,2,3,1,512]{4,0,3,2,1:T(8,128)S(1)}, u32[]{:S(2)}, u32[]{:S(2)}) collective-permute-start(f32[64,2,3,1,512]{4,0,3,2,1:T(8,128)S(1)} %get-tuple-element.170), channel_id=1, source_target_pairs={{1,0},{2,1},{3,2},{4,3},{5,4},{6,5},{7,6},{8,7},{9,8},{10,9},{11,1... | collective-permute-start | bytes 2359304 | tf_op jit(solution)/shard_map/ppermute | solution.py:24
  53.1 14.2 %collective-permute-start.4 = (f32[64,2,3,1,512]{4,0,3,2,1:T(8,128)S(1)}, f32[64,2,3,1,512]{4,0,3,2,1:T(8,128)S(1)}, u32[]{:S(2)}, u32[]{:S(2)}) collective-permute-start(f32[64,2,3,1,512]{4,0,3,2,1:T(8,128)S(1)} %get-tuple-element.171), channel_id=1, source_target_pairs={{0,1},{1,2},{2,3},{3,4},{4,5},{5,6},{6,7},{7,8},{8,9},{9,10},{10,1... | collective-permute-start | bytes 2359304 | tf_op jit(solution)/shard_map/ppermute | solution.py:22
  75.2 1.5 copy-start.4
  76.7 343.0 %copy-start.84 = (s32[2048]{0:T(1024)S(1)}, s32[2048]{0:T(1024)}, u32[]{:S(2)}) copy-start(s32[2048]{0:T(1024)} %pad_clamp_fusion) | copy-start | bytes 24580
  76.7 1.9 copy-start
  118.1 1.5 copy-start.1
  119.7 1.9 copy-start
  161.0 1.5 copy-start.1
  162.5 1.9 copy-start
  203.9 1.5 copy-start.1
  205.4 1.9 copy-start
  246.8 1.5 copy-start.1
  248.3 1.9 copy-start
  289.6 1.5 copy-start.1
  291.1 1.9 copy-start
  332.5 1.5 copy-start.1
  334.0 1.9 copy-start
  375.4 1.5 copy-start.1
  376.9 1.9 copy-start
  418.2 1.5 copy-start.1
  (44 other events, 33.5 us)
Sparse Core Ops, SparseCore 0:
  431.5 61.7 reduce-scatter.1
where the time goes:
time: 502 us; the launch traced here: 500 us
  other arithmetic  217 us (43%)
  local copies, waits for them, and re-layouts  152 us (30%)
  waiting for transfers between devices  73.9 us (15%)
  matrix products  35.8 us (7%)
  between operations  14.6 us (3%)
  starting transfers between devices  6.18 us (1%)
    another operation x8, other arithmetic  108 us
    another operation x16, local copies, waits for them, and re-layouts, diquark_grid(): return jnp.stack([jnp.stack(real_rows, 2), jnp.stack(imag_rows, 2)], 2)  94.4 us
    another operation x8, other arithmetic, diquark_grid(): return jnp.stack([jnp.stack(real_rows, 2), jnp.stack(imag_rows, 2)], 2)  77.6 us
    reduce_scatter x1, waiting for transfers between devices, on_device(): return lax.psum_scatter(placed, 'brick', scatter_dimension=0, tiled=True)  62 us
    dot_general x8, matrix products, elemental_block(): lax.dot_general(left_mat, right_mat, (((1,), (1,)), ((), ())), preferred_...  35.8 us
    dynamic_slice x16, local copies, waits for them, and re-layouts, on_device(): lax.map(one_group, left_groups)  10.3 us
  transfers between devices with their start and end apart: 6, of which 3 were waited for; matrix products, arithmetic and copies ran while one was open for 5% of the time, Pallas kernels for 0%

commit v1 on v0

v1 whole, which is shorter than its diff:
```python
import functools
import math

import jax
import jax.numpy as jnp
import numpy as np
from jax import lax
from jax.experimental import pallas as pl
from jax.experimental.pallas import tpu as pltpu
from jax.sharding import PartitionSpec as P

PB = 32
CAP = 4
LX = 8
LANES = 128
ROWS = 8
VMEM = pl.BlockSpec(memory_space=pltpu.VMEM)
SMEM = pl.BlockSpec(memory_space=pltpu.SMEM)


def params(limit_mib):
    return pltpu.CompilerParams(vmem_limit_bytes=limit_mib * 1024 * 1024)


def cost(flops, bytes_accessed):
    return pl.CostEstimate(
        flops=int(flops), bytes_accessed=int(bytes_accessed), transcendentals=0
    )


def tile_rows(array):
    planes, sites = array.shape[-2:]
    tiles = sites // LANES
    lead = math.prod(array.shape[:-2])
    array = array.reshape(lead, planes, tiles, LANES).transpose(0, 2, 1, 3)
    return array.reshape(lead * tiles * planes, LANES)


def times(link, field, total):
    total = list(total)
    for out_row in range(3):
        for in_row in range(3):
            real, imag = link(0, out_row, in_row), link(1, out_row, in_row)
            f_real, f_imag = field[in_row], field[3 + in_row]
            total[out_row] = total[out_row] + real * f_real - imag * f_imag
            total[3 + out_row] = total[3 + out_row] + real * f_imag + imag * f_real
    return total


def adjoint(link, field, total):
    total = list(total)
    for out_row in range(3):
        for in_row in range(3):
            real, imag = link(0, in_row, out_row), link(1, in_row, out_row)
            f_real, f_imag = field[in_row], field[3 + in_row]
            total[out_row] = total[out_row] + real * f_real + imag * f_imag
            total[3 + out_row] = total[3 + out_row] + real * f_imag - imag * f_real
    return total


def split_kernel(tiles, per_chunk, x_ref, *out_refs):
    vectors = out_refs[0].shape[1]
    chunks = tiles // per_chunk
    for part in range(6):
        for tile in range(tiles):
            for plane in range(2):
                rows = pl.ds((part * tiles + tile) * 2 + plane, vectors, stride=6 * tiles * 2)
                at = (tile % per_chunk) * LANES
                out_refs[plane * chunks + tile // per_chunk][part, :, at : at + LANES] = x_ref[
                    rows, :
                ]


def local_kernel(tiles, per_chunk, link_ref, *refs):
    chunks = tiles // per_chunk
    fields, totals = refs[: 2 * chunks], refs[2 * chunks :]
    vectors = fields[0].shape[1]
    lane = lax.broadcasted_iota(jnp.int32, (ROWS, LANES), 1)
    column = lane % LX
    first_column, last_column = column == 0, column == LX - 1
    below, above = lane < LX, lane >= LANES - LX
    zeros = [jnp.zeros((ROWS, LANES), jnp.float32)] * 6

    def step(group, carry):
        rows = pl.ds(pl.multiple_of(group * ROWS, ROWS), ROWS)

        def get(plane, tile):
            at = (tile % per_chunk) * LANES
            ref = fields[plane * chunks + tile // per_chunk]
            return [ref[part, rows, at : at + LANES] for part in range(6)]

        def link_of(direction, plane, tile):
            def link(part, row, column_at):
                index = ((direction * 2 + part) * 3 + row) * 3 + column_at
                index = (index * tiles + tile) * 2 + plane
                return link_ref[index : index + 1, :]

            return link

        for plane in range(2):
            sums = []
            rolled_in = []
            rolled_out = []
            for tile in range(tiles):
                field = get(plane, tile)
                ahead = [
                    jnp.where(
                        last_column, pltpu.roll(f, LX - 1, 1), pltpu.roll(f, LANES - 1, 1)
                    )
                    for f in field
                ]
                behind = adjoint(link_of(0, plane, tile), field, zeros)
                total = [
                    jnp.where(
                        first_column, pltpu.roll(f, LANES - LX + 1, 1), pltpu.roll(f, 1, 1)
                    )
                    for f in behind
                ]
                total = times(link_of(0, plane, tile), ahead, total)
                if plane == 0:
                    total = times(link_of(2, 0, tile), get(1, tile), total)
                else:
                    total = adjoint(link_of(2, 0, tile), get(0, tile), total)
                sums.append(total)
                rolled_in.append([pltpu.roll(f, LANES - LX, 1) for f in field])
                rolled_out.append(
                    [
                        pltpu.roll(f, LX, 1)
                        for f in adjoint(link_of(1, plane, tile), field, zeros)
                    ]
                )
            for tile in range(tiles):
                after, before = (tile + 1) % tiles, (tile - 1) % tiles
                ahead = [
                    jnp.where(above, b, a) for a, b in zip(rolled_in[tile], rolled_in[after])
                ]
                total = times(link_of(1, plane, tile), ahead, sums[tile])
                at = (tile % per_chunk) * LANES
                out = totals[plane * chunks + tile // per_chunk]
                for part in range(6):
                    back = jnp.where(below, rolled_out[before][part], rolled_out[tile][part])
                    out[part, rows, at : at + LANES] = total[part] + back
        return carry

    lax.fori_loop(0, vectors // ROWS, step, 0)


def outer_hops(tiles, first_tile, link_ref, low_ref, lower, upper, part_sums, rows, at, tile):
    def up(part, row, column_at):
        index = ((2 * 2 + part) * 3 + row) * 3 + column_at
        index = (index * tiles + first_tile + tile) * 2 + 1
        return link_ref[index : index + 1, :]

    def down(part, row, column_at):
        index = (part * 3 + row) * 3 + column_at
        index = index * tiles + first_tile + tile
        return low_ref[index : index + 1, :]

    def get(ref):
        return [ref[part, rows, at : at + LANES] for part in range(6)]

    return (
        adjoint(down, get(lower), get(part_sums[0])),
        times(up, get(upper), get(part_sums[1])),
    )


def edge_kernel(
    tiles, first_tile, link_ref, low_ref, lower, upper, sum_0, sum_1, out_0, out_1
):
    vectors, width = lower.shape[1:]

    def step(group, carry):
        rows = pl.ds(pl.multiple_of(group * ROWS, ROWS), ROWS)
        for tile in range(width // LANES):
            at = tile * LANES
            found = outer_hops(
                tiles, first_tile, link_ref, low_ref, lower, upper, (sum_0, sum_1), rows, at, tile
            )
            for plane, out in enumerate((out_0, out_1)):
                for part in range(6):
                    out[part, rows, at : at + LANES] = found[plane][part] * (1.0 / 6.0)
        return carry

    lax.fori_loop(0, vectors // ROWS, step, 0)


def pair_tiles(vectors):
    groups = vectors // ROWS
    return [(left, right) for right in range(groups) for left in range(right + 1)]


def chunk_sums(
    tiles, first_tile, link_ref, low_ref, lower, upper, sum_0, sum_1, own_0, own_1, field, low,
    quarks, store,
):
    vectors, width = lower.shape[1:]

    def filter_step(group, carry):
        rows = pl.ds(pl.multiple_of(group * ROWS, ROWS), ROWS)
        for tile in range(width // LANES):
            at = tile * LANES
            found = outer_hops(
                tiles, first_tile, link_ref, low_ref, lower, upper, (sum_0, sum_1), rows, at, tile
            )
            for plane, own in enumerate((own_0, own_1)):
                for part in range(6):
                    field[plane * 6 + part, rows, at : at + LANES] = (
                        found[plane][part] * (2.0 / 6.0) - own[part, rows, at : at + LANES]
                    )
        return carry

    lax.fori_loop(0, vectors // ROWS, filter_step, 0)

    for plane in range(2):
        for colour in range(3):
            real = field[plane * 6 + colour].astype(jnp.bfloat16)
            imag = field[plane * 6 + 3 + colour].astype(jnp.bfloat16)
            for part, (top, bottom) in enumerate(((real, imag), (-imag, real))):
                at = (part * 3 + colour) * width
                low[plane, :vectors, at : at + width] = top
                low[plane, vectors:, at : at + width] = bottom

    combos = pair_tiles(vectors)
    groups = vectors // ROWS
    block = ROWS * ROWS

    def plane_step(plane, carry):
        for right in range(groups):
            base = right * (right + 1) // 2

            def left_step(left, inner):
                start = pl.multiple_of((base + left) * block, block)
                for tile in range(width // LANES):
                    at = tile * LANES

                    def load(part, rows):
                        return field[plane * 6 + part, rows, at : at + LANES]

                    right_rows = pl.ds(right * ROWS, ROWS)
                    left_rows = pl.ds(pl.multiple_of(left * ROWS, ROWS), ROWS)
                    b = [load(part, right_rows) for part in range(6)]
                    group = [
                        field.at[plane * 6 + part, left_rows, at : at + LANES]
                        for part in range(6)
                    ]
                    made = [[] for _ in range(6)]
                    for row in range(ROWS):
                        a = [ref[row : row + 1, :] for ref in group]
                        for colour in range(3):
                            x, y = (colour + 1) % 3, (colour + 2) % 3
                            real = (a[x] * b[y] - a[3 + x] * b[3 + y]) - (
                                a[y] * b[x] - a[3 + y] * b[3 + x]
                            )
                            imag = (a[x] * b[3 + y] + a[3 + x] * b[y]) - (
                                a[y] * b[3 + x] + a[3 + y] * b[x]
                            )
                            made[colour].append(real)
                            made[3 + colour].append(imag)
                    for part in range(6):
                        quarks[pl.ds(start, block), part * width + at : part * width + at + LANES] = (
                            jnp.concatenate(made[part], 0).astype(jnp.bfloat16)
                        )
                return inner

            lax.fori_loop(0, right + 1, left_step, 0)
        store(
            plane,
            lax.dot_general(
                quarks[...],
                low[plane],
                (((1,), (1,)), ((), ())),
                preferred_element_type=jnp.float32,
            ),
        )
        return carry

    lax.fori_loop(0, 2, plane_step, 0)


def first_chunk_kernel(tiles, link_ref, low_ref, *refs):
    ins, out, scratch = refs[:6], refs[6], refs[7:]

    def store(plane, value):
        @pl.when(plane == 0)
        def _():
            out[...] = value

        @pl.when(plane > 0)
        def _():
            out[...] += value

    chunk_sums(tiles, 0, link_ref, low_ref, *ins, *scratch, store)


def last_chunk_kernel(
    tiles, first_tile, factor, place_ref, slot_ref, link_ref, low_ref, *refs
):
    ins, before, keep, send, sums, scratch = (
        refs[:6], refs[6], refs[7], refs[8], refs[9], refs[10:-1],
    )
    ordered = refs[-1]

    def store(plane, value):
        @pl.when(plane == 0)
        def _():
            sums[...] = before[...] + value

        @pl.when(plane > 0)
        def _():
            sums[...] += value

    chunk_sums(tiles, first_tile, link_ref, low_ref, *ins, *scratch, store)
    vectors = ins[0].shape[1]
    for number, (left, right) in enumerate(pair_tiles(vectors)):
        for row in range(ROWS):
            first = left * ROWS + row
            skip = max(0, first + 1 - right * ROWS)
            if skip >= ROWS:
                continue
            second = right * ROWS + skip
            pair = first * vectors - first * (first + 1) // 2 + second - first - 1
            at = (number * ROWS + row) * ROWS
            ordered[pair : pair + ROWS - skip, :] = sums[at + skip : at + ROWS, :] * factor
    keep[...] = jnp.zeros_like(keep)
    send[...] = jnp.zeros_like(send)
    chips = keep.shape[0]
    my_chip, my_core = place_ref[0], place_ref[1]

    def place(block, carry):
        slot = slot_ref[block]
        owner = slot // CAP
        away = lax.rem(owner // 2 - my_chip + chips, chips)
        value = ordered[pl.ds(pl.multiple_of(block * PB, PB), PB), :]

        @pl.when(owner % 2 == my_core)
        def _():
            keep[away, slot % CAP] = value

        @pl.when(owner % 2 != my_core)
        def _():
            send[away, slot % CAP] = value

        return carry

    lax.fori_loop(0, slot_ref.shape[0], place, 0)


def combine_kernel(keep, received, *outs):
    for away, out in enumerate(outs):
        out[...] = keep[away] + received[away]


def total_kernel(*refs):
    total = refs[0][...]
    for ref in refs[1:-1]:
        total = total + ref[...]
    refs[-1][...] = total


def on_device(eigen_vectors, link_field, block_slot):
    count = lax.axis_size("brick")
    vectors, _, _, planes, sites = eigen_vectors.shape
    tiles = sites // LANES
    chunks = 2
    per_chunk = tiles // chunks
    width = per_chunk * LANES
    piece = jax.ShapeDtypeStruct((6, vectors, width), jnp.float32)
    piece_bytes = 6 * vectors * width * 4
    pair_rows = len(pair_tiles(vectors)) * ROWS * ROWS
    upward = [(i, (i + 1) % count) for i in range(count)]
    downward = [((i + 1) % count, i) for i in range(count)]

    links = tile_rows(link_field)
    low_links = lax.ppermute(link_field[2, :, :, :, planes - 1], "brick", upward)
    low_links = low_links.reshape(18 * tiles, LANES)

    own = pl.pallas_call(
        functools.partial(split_kernel, tiles, per_chunk),
        out_shape=[piece] * (2 * chunks),
        in_specs=[VMEM],
        out_specs=[VMEM] * (2 * chunks),
        compiler_params=params(32),
        name="split",
    )(tile_rows(eigen_vectors))

    def exchange(fields):
        lower = [lax.ppermute(fields[chunks + c], "brick", upward) for c in range(chunks)]
        upper = [lax.ppermute(fields[c], "brick", downward) for c in range(chunks)]
        return lower, upper

    def local_hops(fields):
        return pl.pallas_call(
            functools.partial(local_kernel, tiles, per_chunk),
            out_shape=[piece] * (2 * chunks),
            in_specs=[VMEM] * (1 + 2 * chunks),
            out_specs=[VMEM] * (2 * chunks),
            compiler_params=params(48),
            cost_estimate=cost(5e9, 4 * chunks * piece_bytes),
            name="local",
        )(links, *fields)

    lower, upper = exchange(own)
    sums = local_hops(own)
    first = [None] * (2 * chunks)
    for c in range(chunks):
        first[c], first[chunks + c] = pl.pallas_call(
            functools.partial(edge_kernel, tiles, c * per_chunk),
            out_shape=[piece] * 2,
            in_specs=[VMEM] * 6,
            out_specs=[VMEM] * 2,
            compiler_params=params(32),
            name="edge",
        )(links, low_links, lower[c], upper[c], sums[c], sums[chunks + c])

    lower, upper = exchange(first)
    sums = local_hops(first)
    scratch = [
        pltpu.VMEM((12, vectors, width), jnp.float32),
        pltpu.VMEM((2, 2 * vectors, 6 * width), jnp.bfloat16),
        pltpu.VMEM((pair_rows, 6 * width), jnp.bfloat16),
    ]
    partial_sums = jax.ShapeDtypeStruct((pair_rows, 2 * vectors), jnp.float32)
    before = pl.pallas_call(
        functools.partial(first_chunk_kernel, tiles),
        out_shape=partial_sums,
        in_specs=[VMEM] * 8,
        out_specs=VMEM,
        scratch_shapes=scratch,
        compiler_params=params(48),
        cost_estimate=cost(8e9, 6 * piece_bytes),
        name="pairs",
    )(links, low_links, lower[0], upper[0], sums[0], sums[chunks], own[0], own[chunks])
    factor = 1.0 / math.sqrt(3.0 * sites * planes * count)
    me = lax.axis_index("brick")
    chips = count // 2
    place = jnp.stack([me // 2, me % 2]).astype(jnp.int32)
    half = jax.ShapeDtypeStruct((chips, CAP, PB, 2 * vectors), jnp.float32)
    blocks = vectors * (vectors - 1) // 2
    c = chunks - 1
    keep, send = pl.pallas_call(
        functools.partial(last_chunk_kernel, tiles, c * per_chunk, factor),
        out_shape=[half] * 2,
        in_specs=[SMEM] * 2 + [VMEM] * 9,
        out_specs=[VMEM] * 2,
        scratch_shapes=[pltpu.VMEM((pair_rows, 2 * vectors), jnp.float32)]
        + scratch
        + [pltpu.VMEM((blocks, 2 * vectors), jnp.float32)],
        compiler_params=params(48),
        cost_estimate=cost(8e9, 6 * piece_bytes),
        name="last_pairs",
    )(
        place, block_slot, links, low_links, lower[c], upper[c], sums[c], sums[chunks + c],
        own[c], own[chunks + c], before,
    )
    received = lax.ppermute(send, "brick", [(i, i ^ 1) for i in range(count)])
    share = jax.ShapeDtypeStruct((CAP, PB, 2 * vectors), jnp.float32)
    shares = pl.pallas_call(
        combine_kernel,
        out_shape=[share] * chips,
        in_specs=[VMEM] * 2,
        out_specs=[VMEM] * chips,
        compiler_params=params(32),
        name="combine",
    )(keep, received)
    arrived = [shares[0]] + [
        lax.ppermute(
            shares[away],
            "brick",
            [(i, ((i // 2 + away) % chips) * 2 + i % 2) for i in range(count)],
        )
        for away in range(1, chips)
    ]
    return pl.pallas_call(
        total_kernel,
        out_shape=share,
        in_specs=[VMEM] * chips,
        out_specs=VMEM,
        compiler_params=params(32),
        name="total",
    )(*arrived)


def solution(mesh):
    return jax.shard_map(
        on_device,
        mesh=mesh,
        in_specs=(
            P(None, None, None, ("cuts", "brick"), None),
            P(None, None, None, None, ("cuts", "brick"), None),
            P(),
        ),
        out_specs=P(("cuts", "brick"), None, None),
        check_vma=False,
    )
```

time: 502 us -> 88.1 us (0.18)
  other arithmetic: 217 us -> 0.08 us
  local copies, waits for them, and re-layouts: 152 us -> 1.51 us
  waiting for transfers between devices: 73.9 us -> 5.64 us
  Pallas kernels: 0 us -> 41.9 us
  matrix products: 35.8 us -> 0 us
  starting transfers between devices: 6.18 us -> 38.6 us
  between operations: 14.6 us -> 0.17 us
    another operation x48 -> x1, other arithmetic: 191 us -> 0.08 us  [on_device(): place = jnp.stack([me // 2, me % 2]).astype(jnp.int32)]
    another operation x16 -> x0, local copies, waits for them, and re-layouts: 94.4 us -> none  [diquark_grid(): return jnp.stack([jnp.stack(real_rows, 2), jnp.stack(imag_rows, 2)], 2)]
    reduce_scatter x1 -> x0, waiting for transfers between devices: 62 us -> none  [on_device(): return lax.psum_scatter(placed, 'brick', scatter_dimension=0, tiled=True)]
    pallas_call x0 -> x9, Pallas kernels: none -> 41.9 us  [the longest x1 16 us: on_device(): pl.pallas_call(functools.partial(last_chunk_kernel, tiles, c * per_chunk,...]
    dot_general x8 -> x0, matrix products: 35.8 us -> none  [elemental_block(): lax.dot_general(left_mat, right_mat, (((1,), (1,)), ((), ())), preferred_...]
    ppermute x5 -> x17, starting transfers between devices: 6.18 us -> 38.6 us  [the longest x4 12.4 us: exchange(): lax.ppermute(fields[chunks + c], 'brick', upward)]
    dynamic_slice x16 -> x0, local copies, waits for them, and re-layouts: 10.3 us -> none  [on_device(): lax.map(one_group, left_groups)]
    sub x26 -> x0, other arithmetic: 9.45 us -> none  [the longest x18 9.15 us: link_times(): real_part + link_set[0, out_row, in_row] * lattice_field[:, 0, in_row]]
  transfers between devices with their start and end apart: 6 -> 17, of which waited for: 3 -> 4; matrix products, arithmetic and copies ran while one was open for 5% -> 0% of each run, Pallas kernels for 0% -> 27%
where the time goes in v1:
time: 88.1 us; the launch traced here: 87.9 us
  Pallas kernels  41.9 us (48%)
  starting transfers between devices  38.6 us (44%)
  waiting for transfers between devices  5.64 us (6%)
  local copies, waits for them, and re-layouts  1.51 us (2%)
    pallas_call x1, Pallas kernels, on_device(): pl.pallas_call(functools.partial(last_chunk_kernel, tiles, c * per_chunk,...  16 us
    pallas_call x1, Pallas kernels, on_device(): pl.pallas_call(functools.partial(first_chunk_kernel, tiles), out_shape=pa...  13.8 us
    ppermute x4, starting transfers between devices, exchange(): lax.ppermute(fields[chunks + c], 'brick', upward)  12.4 us
    ppermute x7, starting transfers between devices, on_device(): lax.ppermute(shares[away], 'brick', [(i, (i // 2 + away) % chips * 2 + i...  12.4 us
    ppermute x4, starting transfers between devices, exchange(): upper = [lax.ppermute(fields[c], 'brick', downward) for c in range(chunks)]  9.88 us
    pallas_call x2, Pallas kernels, local_hops(): pl.pallas_call(functools.partial(local_kernel, tiles, per_chunk), out_sha...  8.86 us
    ppermute x7, waiting for transfers between devices, on_device(): lax.ppermute(shares[away], 'brick', [(i, (i // 2 + away) % chips * 2 + i...  4.08 us
    ppermute x1, starting transfers between devices, on_device(): received = lax.ppermute(send, 'brick', [(i, i ^ 1) for i in range(count)])  3.91 us
  transfers between devices with their start and end apart: 17, of which 4 were waited for; matrix products, arithmetic and copies ran while one was open for 0% of the time, Pallas kernels for 27%

profile of v1, /device:TPU:0, one launch (start us, length us, event | category | flops | bytes accessed | tf_op | source)
XLA Modules:
  0.0 87.9 jit_solution(2477506475650847518)
XLA Ops:
  0.0 0.0 copy-start
  0.0 1.4 %copy-done = f32[64,2,3,2,512]{4,3,2,1,0:T(2,128)S(1)} copy-done((f32[64,2,3,2,512]{4,3,2,1,0:T(2,128)S(1)}, f32[64,2,3,2,512]{4,3,2,1,0:T(2,128)}, u32[]{:S(2)}) %copy-start) | copy-done | bytes 1572888
  1.4 0.0 copy-start.1
  1.4 1.7 %split.1 = (f32[6,64,256]{2,1,0:T(8,128)}, f32[6,64,256]{2,1,0:T(8,128)}, f32[6,64,256]{2,1,0:T(8,128)}, f32[6,64,256]{2,1,0:T(8,128)}) custom-call(f32[3072,128]{1,0:T(8,128)S(1)} %bitcast.15), custom_call_target="tpu_custom_call" | custom-call | tf_op jit(solution)/shard_map/split/pallas_call | solution.py:378
  3.1 0.5 collective-permute-start.5
  3.5 5.0 %collective-permute-start.6 = (f32[6,64,256]{2,1,0:T(8,128)}, f32[6,64,256]{2,1,0:T(8,128)S(1)}, u32[]{:S(2)}, u32[]{:S(2)}) collective-permute-start(f32[6,64,256]{2,1,0:T(8,128)} %get-tuple-element.33.refs_0_.refs_4_), channel_id=1, source_target_pairs={{1,0},{2,1},{3,2},{4,3},{5,4},{6,5},{7,6},{8,7},{9,8},{10,9},{11,1... | collective-permute-start | bytes 1179656 | tf_op jit(solution)/shard_map/ppermute | solution.py:389
  8.5 0.0 copy-done.1
  8.6 0.1 collective-permute-start
  8.7 0.1 collective-permute-start.1
  8.7 4.4 %collective-permute-start.2 = (f32[6,64,256]{2,1,0:T(8,128)}, f32[6,64,256]{2,1,0:T(8,128)S(1)}, u32[]{:S(2)}, u32[]{:S(2)}) collective-permute-start(f32[6,64,256]{2,1,0:T(8,128)} %get-tuple-element.32.refs_1_.refs_4_), channel_id=1, source_target_pairs={{1,0},{2,1},{3,2},{4,3},{5,4},{6,5},{7,6},{8,7},{9,8},{10,9},{11,1... | collective-permute-start | bytes 1179656 | tf_op jit(solution)/shard_map/ppermute | solution.py:389
  13.1 5.1 %local.2 = (f32[6,64,256]{2,1,0:T(8,128)S(1)}, f32[6,64,256]{2,1,0:T(8,128)S(1)}, f32[6,64,256]{2,1,0:T(8,128)S(1)}, f32[6,64,256]{2,1,0:T(8,128)S(1)}) custom-call(f32[432,128]{1,0:T(8,128)S(1)} %bitcast.16, f32[6,64,256]{2,1,0:T(8,128)} %get-tuple-element.33.refs_0_.refs_4_, f32[6,64,256]{2,1,0:T(8,128)} %get-tuple-element.32.refs_1_.refs_4_, ...), custom_call_target="tpu_custom_call" | custom-call | flops 5000000000 | bytes 3145728 | tf_op jit(solution)/shard_map/local/pallas_call | solution.py:393
  18.2 0.1 pad_add_fusion.place_ref
  18.3 0.0 collective-permute-done
  18.4 0.0 collective-permute-done.5.lower
  18.4 0.0 collective-permute-done.6.upper
  18.4 0.4 edge.3
  18.8 4.0 %collective-permute-start.7 = (f32[6,64,256]{2,1,0:T(8,128)S(1)}, f32[6,64,256]{2,1,0:T(8,128)S(1)}, u32[]{:S(2)}, u32[]{:S(2)}) collective-permute-start(f32[6,64,256]{2,1,0:T(8,128)S(1)} %get-tuple-element.42.refs_2_), channel_id=1, source_target_pairs={{0,1},{1,2},{2,3},{3,4},{4,5},{5,6},{6,7},{7,8},{8,9},{9,10},{10,1... | collective-permute-start | bytes 1179656 | tf_op jit(solution)/shard_map/ppermute | solution.py:388
  22.9 0.5 collective-permute-start.8
  23.3 0.0 collective-permute-done.1.lower
  23.3 0.0 collective-permute-done.2.upper
  23.3 0.4 edge.2
  23.7 7.9 %collective-permute-start.3 = (f32[6,64,256]{2,1,0:T(8,128)S(1)}, f32[6,64,256]{2,1,0:T(8,128)S(1)}, u32[]{:S(2)}, u32[]{:S(2)}) collective-permute-start(f32[6,64,256]{2,1,0:T(8,128)S(1)} %get-tuple-element.37.refs_3_), channel_id=1, source_target_pairs={{0,1},{1,2},{2,3},{3,4},{4,5},{5,6},{6,7},{7,8},{8,9},{9,10},{10,1... | collective-permute-start | bytes 1179656 | tf_op jit(solution)/shard_map/ppermute | solution.py:388
  31.6 0.0 collective-permute-start.4
  31.6 3.8 %local.3 = (f32[6,64,256]{2,1,0:T(8,128)S(1)}, f32[6,64,256]{2,1,0:T(8,128)S(1)}, f32[6,64,256]{2,1,0:T(8,128)S(1)}, f32[6,64,256]{2,1,0:T(8,128)S(1)}) custom-call(f32[432,128]{1,0:T(8,128)S(1)} %bitcast.19, f32[6,64,256]{2,1,0:T(8,128)S(1)} %get-tuple-element.41.refs_0_, f32[6,64,256]{2,1,0:T(8,128)S(1)} %get-tuple-element.38.refs_1_, ...), custom_call_target="tpu_custom_call" | custom-call | flops 5000000000 | bytes 3145728 | tf_op jit(solution)/shard_map/local/pallas_call | solution.py:393
  35.4 0.0 collective-permute-done.7.refs_0_
  35.4 0.0 collective-permute-done.8.refs_1_
  35.4 0.0 copy-start.2
  35.4 13.8 %pairs.1.refs_6_ = f32[2304,128]{1,0:T(8,128)S(1)} custom-call(f32[432,128]{1,0:T(8,128)S(1)} %bitcast.20, f32[72,128]{1,0:T(8,128)S(1)} %reshape.17.low_ref, f32[6,64,256]{2,1,0:T(8,128)S(1)} %collective-permute-done.7.refs_0_, f32[6,64,256]{2,1,0:T(8,128)S(1)} %collective-permute-done.8.refs_1_, f32[6,64,256]{2,1,0:T(8,128)S(1)} %get-tuple-element.45.refs_2_, ...), custom_call_target="tpu_custom_call" | custom-call | flops 8000000000 | bytes 2359296 | tf_op jit(solution)/shard_map/pairs/pallas_call | solution.py:424
  49.2 0.0 collective-permute-done.3.refs_0_
  49.2 0.0 collective-permute-done.4.refs_1_
  49.2 0.0 copy-done.2
  49.3 16.0 %last_pairs.1 = (f32[8,4,32,128]{3,2,1,0:T(8,128)S(1)}, f32[8,4,32,128]{3,2,1,0:T(8,128)S(1)}) custom-call(s32[2]{0:T(128)S(1)} %pad_add_fusion.place_ref, s32[63]{0:T(128)S(1)} %copy-done.2, f32[432,128]{1,0:T(8,128)S(1)} %bitcast.21, f32[72,128]{1,0:T(8,128)S(1)} %reshape.17.low_ref, f32[6,64,256]{2,1,0:T(8,128)S(1)} %collective-permute-done.3.refs_0_, ...), custom_call_target="tpu_custom_call" | custom-call | flops 8000000000 | bytes 2359296 | tf_op jit(solution)/shard_map/last_pairs/pallas_call | solution.py:441
  65.3 3.9 %collective-permute-start.9 = (f32[8,4,32,128]{3,2,1,0:T(8,128)S(1)}, f32[8,4,32,128]{3,2,1,0:T(8,128)S(1)}, u32[]{:S(2)}, u32[]{:S(2)}) collective-permute-start(f32[8,4,32,128]{3,2,1,0:T(8,128)S(1)} %get-tuple-element.48), channel_id=1, source_target_pairs={{0,1},{1,0},{2,3},{3,2},{4,5},{5,4},{6,7},{7,6},{8,9},{9,8},{10,11... | collective-permute-start | bytes 1572872 | tf_op jit(solution)/shard_map/ppermute | solution.py:456
  69.2 1.5 %collective-permute-done.9.received = f32[8,4,32,128]{3,2,1,0:T(8,128)S(1)} collective-permute-done((f32[8,4,32,128]{3,2,1,0:T(8,128)S(1)}, f32[8,4,32,128]{3,2,1,0:T(8,128)S(1)}, u32[]{:S(2)}, u32[]{:S(2)}) %collective-permute-start.9) | collective-permute-done | bytes 524320 | tf_op jit(solution)/shard_map/ppermute | solution.py:456
  70.7 0.1 combine.1
  70.8 0.1 collective-permute-start.10
  70.9 4.3 %collective-permute-start.11 = (f32[4,32,128]{2,1,0:T(8,128)S(1)}, f32[4,32,128]{2,1,0:T(8,128)S(1)}, u32[]{:S(2)}, u32[]{:S(2)}) collective-permute-start(f32[4,32,128]{2,1,0:T(8,128)S(1)} %get-tuple-element.51), channel_id=1, source_target_pairs={{0,4},{1,5},{2,6},{3,7},{4,8},{5,9},{6,10},{7,11},{8,12},{9,13},{1... | collective-permute-start | bytes 196616 | tf_op jit(solution)/shard_map/ppermute | solution.py:467
  75.2 1.1 %collective-permute-start.12 = (f32[4,32,128]{2,1,0:T(8,128)S(1)}, f32[4,32,128]{2,1,0:T(8,128)S(1)}, u32[]{:S(2)}, u32[]{:S(2)}) collective-permute-start(f32[4,32,128]{2,1,0:T(8,128)S(1)} %get-tuple-element.52), channel_id=1, source_target_pairs={{0,6},{1,7},{2,8},{3,9},{4,10},{5,11},{6,12},{7,13},{8,14},{9,15},... | collective-permute-start | bytes 196616 | tf_op jit(solution)/shard_map/ppermute | solution.py:467
  76.3 1.5 %collective-permute-start.13 = (f32[4,32,128]{2,1,0:T(8,128)S(1)}, f32[4,32,128]{2,1,0:T(8,128)S(1)}, u32[]{:S(2)}, u32[]{:S(2)}) collective-permute-start(f32[4,32,128]{2,1,0:T(8,128)S(1)} %get-tuple-element.53), channel_id=1, source_target_pairs={{0,8},{1,9},{2,10},{3,11},{4,12},{5,13},{6,14},{7,15},{8,0},{9,1},... | collective-permute-start | bytes 196616 | tf_op jit(solution)/shard_map/ppermute | solution.py:467
  77.8 2.3 %collective-permute-start.14 = (f32[4,32,128]{2,1,0:T(8,128)S(1)}, f32[4,32,128]{2,1,0:T(8,128)S(1)}, u32[]{:S(2)}, u32[]{:S(2)}) collective-permute-start(f32[4,32,128]{2,1,0:T(8,128)S(1)} %get-tuple-element.54), channel_id=1, source_target_pairs={{0,10},{1,11},{2,12},{3,13},{4,14},{5,15},{6,0},{7,1},{8,2},{9,3},... | collective-permute-start | bytes 196616 | tf_op jit(solution)/shard_map/ppermute | solution.py:467
  80.1 0.0 collective-permute-done.10.refs_1_
  80.1 2.9 %collective-permute-start.15 = (f32[4,32,128]{2,1,0:T(8,128)S(1)}, f32[4,32,128]{2,1,0:T(8,128)S(1)}, u32[]{:S(2)}, u32[]{:S(2)}) collective-permute-start(f32[4,32,128]{2,1,0:T(8,128)S(1)} %get-tuple-element.55), channel_id=1, source_target_pairs={{0,12},{1,13},{2,14},{3,15},{4,0},{5,1},{6,2},{7,3},{8,4},{9,5},{1... | collective-permute-start | bytes 196616 | tf_op jit(solution)/shard_map/ppermute | solution.py:467
  83.0 0.0 collective-permute-done.11.refs_2_
  83.0 0.2 collective-permute-start.16
  83.2 1.3 %collective-permute-done.12.refs_3_ = f32[4,32,128]{2,1,0:T(8,128)S(1)} collective-permute-done((f32[4,32,128]{2,1,0:T(8,128)S(1)}, f32[4,32,128]{2,1,0:T(8,128)S(1)}, u32[]{:S(2)}, u32[]{:S(2)}) %collective-permute-start.12) | collective-permute-done | bytes 65568 | tf_op jit(solution)/shard_map/ppermute | solution.py:467
  84.5 0.0 collective-permute-done.13.refs_4_
  84.5 0.0 collective-permute-done.14.refs_5_
  84.5 2.0 %collective-permute-done.15.refs_6_ = f32[4,32,128]{2,1,0:T(8,128)S(1)} collective-permute-done((f32[4,32,128]{2,1,0:T(8,128)S(1)}, f32[4,32,128]{2,1,0:T(8,128)S(1)}, u32[]{:S(2)}, u32[]{:S(2)}) %collective-permute-start.15) | collective-permute-done | bytes 65568 | tf_op jit(solution)/shard_map/ppermute | solution.py:467
  86.5 0.8 collective-permute-done.16.refs_7_
  87.3 0.7 total.1
  (4 shorter events, 0.1 us)
Async XLA Ops:
  0.0 1.4 %copy-start = (f32[64,2,3,2,512]{4,3,2,1,0:T(2,128)S(1)}, f32[64,2,3,2,512]{4,3,2,1,0:T(2,128)}, u32[]{:S(2)}) copy-start(f32[64,2,3,2,512]{4,3,2,1,0:T(2,128)} %param.3) | copy-start | bytes 4718596
  1.4 7.1 %copy-start.1 = (f32[3,2,3,3,2,512]{5,4,3,2,1,0:T(2,128)S(1)}, f32[3,2,3,3,2,512]{5,4,3,2,1,0:T(2,128)}, u32[]{:S(2)}) copy-start(f32[3,2,3,3,2,512]{5,4,3,2,1,0:T(2,128)} %param.4) | copy-start | bytes 663556
  3.1 15.3 %collective-permute-start.5 = (f32[6,64,256]{2,1,0:T(8,128)}, f32[6,64,256]{2,1,0:T(8,128)S(1)}, u32[]{:S(2)}, u32[]{:S(2)}) collective-permute-start(f32[6,64,256]{2,1,0:T(8,128)} %get-tuple-element.34.refs_2_.refs_5_), channel_id=1, source_target_pairs={{0,1},{1,2},{2,3},{3,4},{4,5},{5,6},{6,7},{7,8},{8,9},{9,10},{10,1... | collective-permute-start | bytes 1179656 | tf_op jit(solution)/shard_map/ppermute | solution.py:388
  3.5 14.9 %collective-permute-start.6 = (f32[6,64,256]{2,1,0:T(8,128)}, f32[6,64,256]{2,1,0:T(8,128)S(1)}, u32[]{:S(2)}, u32[]{:S(2)}) collective-permute-start(f32[6,64,256]{2,1,0:T(8,128)} %get-tuple-element.33.refs_0_.refs_4_), channel_id=1, source_target_pairs={{1,0},{2,1},{3,2},{4,3},{5,4},{6,5},{7,6},{8,7},{9,8},{10,9},{11,1... | collective-permute-start | bytes 1179656 | tf_op jit(solution)/shard_map/ppermute | solution.py:389
  8.6 9.7 %collective-permute-start = (f32[2,3,3,512]{3,0,2,1:T(2,128)S(1)}, f32[2,3,3,512]{3,0,2,1:T(2,128)S(1)}, u32[]{:S(2)}, u32[]{:S(2)}) collective-permute-start(f32[2,3,3,512]{3,0,2,1:T(2,128)S(1)} %bitcast.22), channel_id=1, source_target_pairs={{0,1},{1,2},{2,3},{3,4},{4,5},{5,6},{6,7},{7,8},{8,9},{9,10},{10,1... | collective-permute-start | bytes 110600 | tf_op jit(solution)/shard_map/ppermute | solution.py:375
  8.7 14.7 %collective-permute-start.1 = (f32[6,64,256]{2,1,0:T(8,128)}, f32[6,64,256]{2,1,0:T(8,128)S(1)}, u32[]{:S(2)}, u32[]{:S(2)}) collective-permute-start(f32[6,64,256]{2,1,0:T(8,128)} %get-tuple-element.31.refs_3_.refs_5_), channel_id=1, source_target_pairs={{0,1},{1,2},{2,3},{3,4},{4,5},{5,6},{6,7},{7,8},{8,9},{9,10},{10,1... | collective-permute-start | bytes 1179656 | tf_op jit(solution)/shard_map/ppermute | solution.py:388
  8.7 14.6 %collective-permute-start.2 = (f32[6,64,256]{2,1,0:T(8,128)}, f32[6,64,256]{2,1,0:T(8,128)S(1)}, u32[]{:S(2)}, u32[]{:S(2)}) collective-permute-start(f32[6,64,256]{2,1,0:T(8,128)} %get-tuple-element.32.refs_1_.refs_4_), channel_id=1, source_target_pairs={{1,0},{2,1},{3,2},{4,3},{5,4},{6,5},{7,6},{8,7},{9,8},{10,9},{11,1... | collective-permute-start | bytes 1179656 | tf_op jit(solution)/shard_map/ppermute | solution.py:389
  18.8 16.6 %collective-permute-start.7 = (f32[6,64,256]{2,1,0:T(8,128)S(1)}, f32[6,64,256]{2,1,0:T(8,128)S(1)}, u32[]{:S(2)}, u32[]{:S(2)}) collective-permute-start(f32[6,64,256]{2,1,0:T(8,128)S(1)} %get-tuple-element.42.refs_2_), channel_id=1, source_target_pairs={{0,1},{1,2},{2,3},{3,4},{4,5},{5,6},{6,7},{7,8},{8,9},{9,10},{10,1... | collective-permute-start | bytes 1179656 | tf_op jit(solution)/shard_map/ppermute | solution.py:388
  22.9 12.5 %collective-permute-start.8 = (f32[6,64,256]{2,1,0:T(8,128)S(1)}, f32[6,64,256]{2,1,0:T(8,128)S(1)}, u32[]{:S(2)}, u32[]{:S(2)}) collective-permute-start(f32[6,64,256]{2,1,0:T(8,128)S(1)} %get-tuple-element.41.refs_0_), channel_id=1, source_target_pairs={{1,0},{2,1},{3,2},{4,3},{5,4},{6,5},{7,6},{8,7},{9,8},{10,9},{11,1... | collective-permute-start | bytes 1179656 | tf_op jit(solution)/shard_map/ppermute | solution.py:389
  23.7 25.5 %collective-permute-start.3 = (f32[6,64,256]{2,1,0:T(8,128)S(1)}, f32[6,64,256]{2,1,0:T(8,128)S(1)}, u32[]{:S(2)}, u32[]{:S(2)}) collective-permute-start(f32[6,64,256]{2,1,0:T(8,128)S(1)} %get-tuple-element.37.refs_3_), channel_id=1, source_target_pairs={{0,1},{1,2},{2,3},{3,4},{4,5},{5,6},{6,7},{7,8},{8,9},{9,10},{10,1... | collective-permute-start | bytes 1179656 | tf_op jit(solution)/shard_map/ppermute | solution.py:388
  31.6 17.6 %collective-permute-start.4 = (f32[6,64,256]{2,1,0:T(8,128)S(1)}, f32[6,64,256]{2,1,0:T(8,128)S(1)}, u32[]{:S(2)}, u32[]{:S(2)}) collective-permute-start(f32[6,64,256]{2,1,0:T(8,128)S(1)} %get-tuple-element.38.refs_1_), channel_id=1, source_target_pairs={{1,0},{2,1},{3,2},{4,3},{5,4},{6,5},{7,6},{8,7},{9,8},{10,9},{11,1... | collective-permute-start | bytes 1179656 | tf_op jit(solution)/shard_map/ppermute | solution.py:389
  35.4 13.9 %copy-start.2 = (s32[63]{0:T(128)S(1)}, s32[63]{0:T(128)}, u32[]{:S(2)}) copy-start(s32[63]{0:T(128)} %slot_ref.1) | copy-start | bytes 760
  65.3 5.4 %collective-permute-start.9 = (f32[8,4,32,128]{3,2,1,0:T(8,128)S(1)}, f32[8,4,32,128]{3,2,1,0:T(8,128)S(1)}, u32[]{:S(2)}, u32[]{:S(2)}) collective-permute-start(f32[8,4,32,128]{3,2,1,0:T(8,128)S(1)} %get-tuple-element.48), channel_id=1, source_target_pairs={{0,1},{1,0},{2,3},{3,2},{4,5},{5,4},{6,7},{7,6},{8,9},{9,8},{10,11... | collective-permute-start | bytes 1572872 | tf_op jit(solution)/shard_map/ppermute | solution.py:456
  70.8 9.3 %collective-permute-start.10 = (f32[4,32,128]{2,1,0:T(8,128)S(1)}, f32[4,32,128]{2,1,0:T(8,128)S(1)}, u32[]{:S(2)}, u32[]{:S(2)}) collective-permute-start(f32[4,32,128]{2,1,0:T(8,128)S(1)} %get-tuple-element.50), channel_id=1, source_target_pairs={{0,2},{1,3},{2,4},{3,5},{4,6},{5,7},{6,8},{7,9},{8,10},{9,11},{10,... | collective-permute-start | bytes 196616 | tf_op jit(solution)/shard_map/ppermute | solution.py:467
  70.9 12.1 %collective-permute-start.11 = (f32[4,32,128]{2,1,0:T(8,128)S(1)}, f32[4,32,128]{2,1,0:T(8,128)S(1)}, u32[]{:S(2)}, u32[]{:S(2)}) collective-permute-start(f32[4,32,128]{2,1,0:T(8,128)S(1)} %get-tuple-element.51), channel_id=1, source_target_pairs={{0,4},{1,5},{2,6},{3,7},{4,8},{5,9},{6,10},{7,11},{8,12},{9,13},{1... | collective-permute-start | bytes 196616 | tf_op jit(solution)/shard_map/ppermute | solution.py:467
  75.2 9.2 %collective-permute-start.12 = (f32[4,32,128]{2,1,0:T(8,128)S(1)}, f32[4,32,128]{2,1,0:T(8,128)S(1)}, u32[]{:S(2)}, u32[]{:S(2)}) collective-permute-start(f32[4,32,128]{2,1,0:T(8,128)S(1)} %get-tuple-element.52), channel_id=1, source_target_pairs={{0,6},{1,7},{2,8},{3,9},{4,10},{5,11},{6,12},{7,13},{8,14},{9,15},... | collective-permute-start | bytes 196616 | tf_op jit(solution)/shard_map/ppermute | solution.py:467
  76.3 8.1 %collective-permute-start.13 = (f32[4,32,128]{2,1,0:T(8,128)S(1)}, f32[4,32,128]{2,1,0:T(8,128)S(1)}, u32[]{:S(2)}, u32[]{:S(2)}) collective-permute-start(f32[4,32,128]{2,1,0:T(8,128)S(1)} %get-tuple-element.53), channel_id=1, source_target_pairs={{0,8},{1,9},{2,10},{3,11},{4,12},{5,13},{6,14},{7,15},{8,0},{9,1},... | collective-permute-start | bytes 196616 | tf_op jit(solution)/shard_map/ppermute | solution.py:467
  77.8 6.7 %collective-permute-start.14 = (f32[4,32,128]{2,1,0:T(8,128)S(1)}, f32[4,32,128]{2,1,0:T(8,128)S(1)}, u32[]{:S(2)}, u32[]{:S(2)}) collective-permute-start(f32[4,32,128]{2,1,0:T(8,128)S(1)} %get-tuple-element.54), channel_id=1, source_target_pairs={{0,10},{1,11},{2,12},{3,13},{4,14},{5,15},{6,0},{7,1},{8,2},{9,3},... | collective-permute-start | bytes 196616 | tf_op jit(solution)/shard_map/ppermute | solution.py:467
  80.1 6.4 %collective-permute-start.15 = (f32[4,32,128]{2,1,0:T(8,128)S(1)}, f32[4,32,128]{2,1,0:T(8,128)S(1)}, u32[]{:S(2)}, u32[]{:S(2)}) collective-permute-start(f32[4,32,128]{2,1,0:T(8,128)S(1)} %get-tuple-element.55), channel_id=1, source_target_pairs={{0,12},{1,13},{2,14},{3,15},{4,0},{5,1},{6,2},{7,3},{8,4},{9,5},{1... | collective-permute-start | bytes 196616 | tf_op jit(solution)/shard_map/ppermute | solution.py:467
  83.0 4.3 %collective-permute-start.16 = (f32[4,32,128]{2,1,0:T(8,128)S(1)}, f32[4,32,128]{2,1,0:T(8,128)S(1)}, u32[]{:S(2)}, u32[]{:S(2)}) collective-permute-start(f32[4,32,128]{2,1,0:T(8,128)S(1)} %get-tuple-element.56), channel_id=1, source_target_pairs={{0,14},{1,15},{2,0},{3,1},{4,2},{5,3},{6,4},{7,5},{8,6},{9,7},{10,... | collective-permute-start | bytes 196616 | tf_op jit(solution)/shard_map/ppermute | solution.py:467

commit v2 on v1

--- a/solution.py
+++ b/solution.py
@@ -186,8 +186,13 @@
 
 
 def pair_tiles(vectors):
-    groups = vectors // ROWS
-    return [(left, right) for right in range(groups) for left in range(right + 1)]
+    half = vectors // ROWS // 2
+    return [
+        (base + left, base + right)
+        for base in (0, half)
+        for right in range(half)
+        for left in range(right + 1)
+    ]
 
 
 def chunk_sums(
@@ -222,57 +227,60 @@
                 low[plane, vectors:, at : at + width] = bottom
 
     combos = pair_tiles(vectors)
-    groups = vectors // ROWS
     block = ROWS * ROWS
+    steps = 4
+    step_combos = len(combos) // steps
+    step_rows = step_combos * block
+
+    def form(plane, number):
+        left, right = combos[number]
+        for tile in range(width // LANES):
+            at = tile * LANES
+            lanes = slice(at, at + LANES)
+            b = [
+                field[plane * 6 + part, right * ROWS : (right + 1) * ROWS, lanes]
+                for part in range(6)
+            ]
+            for row in range(0, ROWS, 2):
+                made = [[] for _ in range(6)]
+                for index in (left * ROWS + row, left * ROWS + row + 1):
+                    a = [field[plane * 6 + part, index : index + 1, lanes] for part in range(6)]
+                    for colour in range(3):
+                        x, y = (colour + 1) % 3, (colour + 2) % 3
+                        made[colour].append(
+                            (a[x] * b[y] - a[3 + x] * b[3 + y])
+                            - (a[y] * b[x] - a[3 + y] * b[3 + x])
+                        )
+                        made[3 + colour].append(
+                            (a[x] * b[3 + y] + a[3 + x] * b[y])
+                            - (a[y] * b[3 + x] + a[3 + y] * b[x])
+                        )
+                start = number * block + row * ROWS
+                for part in range(6):
+                    quarks[
+                        start : start + 2 * ROWS, part * width + at : part * width + at + LANES
+                    ] = jnp.concatenate(made[part], 0).astype(jnp.bfloat16)
 
     def plane_step(plane, carry):
-        for right in range(groups):
-            base = right * (right + 1) // 2
-
-            def left_step(left, inner):
-                start = pl.multiple_of((base + left) * block, block)
-                for tile in range(width // LANES):
-                    at = tile * LANES
-
-                    def load(part, rows):
-                        return field[plane * 6 + part, rows, at : at + LANES]
-
-                    right_rows = pl.ds(right * ROWS, ROWS)
-                    left_rows = pl.ds(pl.multiple_of(left * ROWS, ROWS), ROWS)
-                    b = [load(part, right_rows) for part in range(6)]
-                    group = [
-                        field.at[plane * 6 + part, left_rows, at : at + LANES]
-                        for part in range(6)
-                    ]
-                    made = [[] for _ in range(6)]
-                    for row in range(ROWS):
-                        a = [ref[row : row + 1, :] for ref in group]
-                        for colour in range(3):
-                            x, y = (colour + 1) % 3, (colour + 2) % 3
-                            real = (a[x] * b[y] - a[3 + x] * b[3 + y]) - (
-                                a[y] * b[x] - a[3 + y] * b[3 + x]
-                            )
-                            imag = (a[x] * b[3 + y] + a[3 + x] * b[y]) - (
-                                a[y] * b[3 + x] + a[3 + y] * b[x]
-                            )
-                            made[colour].append(real)
-                            made[3 + colour].append(imag)
-                    for part in range(6):
-                        quarks[pl.ds(start, block), part * width + at : part * width + at + LANES] = (
-                            jnp.concatenate(made[part], 0).astype(jnp.bfloat16)
-                        )
-                return inner
-
-            lax.fori_loop(0, right + 1, left_step, 0)
-        store(
-            plane,
-            lax.dot_general(
-                quarks[...],
-                low[plane],
-                (((1,), (1,)), ((), ())),
-                preferred_element_type=jnp.float32,
-            ),
-        )
+        def form_step(step):
+            for number in range(step * step_combos, (step + 1) * step_combos):
+                form(plane, number)
+
+        form_step(0)
+        for step in range(steps):
+            if step + 1 < steps:
+                form_step(step + 1)
+            rows = slice(step * step_rows, (step + 1) * step_rows)
+            store(
+                plane,
+                rows,
+                lax.dot_general(
+                    quarks[rows, :],
+                    low[plane],
+                    (((1,), (1,)), ((), ())),
+                    preferred_element_type=jnp.float32,
+                ),
+            )
         return carry
 
     lax.fori_loop(0, 2, plane_step, 0)
@@ -280,48 +288,85 @@
 
 def first_chunk_kernel(tiles, link_ref, low_ref, *refs):
     ins, out, scratch = refs[:6], refs[6], refs[7:]
-
-    def store(plane, value):
-        @pl.when(plane == 0)
-        def _():
-            out[...] = value
-
-        @pl.when(plane > 0)
-        def _():
-            out[...] += value
+    out[...] = jnp.zeros_like(out)
+
+    def store(plane, rows, value):
+        out[rows, :] += value
 
     chunk_sums(tiles, 0, link_ref, low_ref, *ins, *scratch, store)
+
+
+def arrange(sums, grid, crossed, ordered, factor):
+    half = grid.shape[0] // 2
+    side = math.isqrt(half)
+    vectors = 2 * side
+    block = ROWS * ROWS
+    for number, (left, right) in enumerate(pair_tiles(vectors)):
+        for row in range(ROWS):
+            start = number * block + row * ROWS
+            at = (left * ROWS + row) * side + right * ROWS % side
+            grid[at : at + ROWS, :] = sums[start : start + ROWS, :] * factor
+            if left != right:
+                at = (right * ROWS + row) * side + left * ROWS % side
+                grid[at : at + ROWS, :] = (
+                    sums[pl.ds(number * block + row, ROWS, stride=ROWS), :] * -factor
+                )
+    lane = lax.broadcasted_iota(jnp.int32, (side, 2 * vectors), 1)
+    own_half = lane % vectors < side
+    per = 2 * vectors // side
+    for start in range(0, half, 2 * vectors):
+        turned = grid[half + start : half + start + 2 * vectors, :].T
+        real, imag = turned[:side], turned[vectors : vectors + side]
+        for index in range(per):
+            second = start // side + index
+            turn = (side - index * side) % (2 * vectors)
+            value = jnp.where(
+                lane < vectors,
+                pltpu.roll(real, turn, 1) if turn else real,
+                pltpu.roll(imag, (turn + vectors) % (2 * vectors), 1)
+                if (turn + vectors) % (2 * vectors)
+                else imag,
+            )
+            crossed[pl.ds(second, side, stride=side), :] = value
+    for start in range(0, half, 2 * vectors):
+        turned = grid[start : start + 2 * vectors, :].T
+        real, imag = turned[side:vectors], turned[vectors + side :]
+        for index in range(per):
+            first = start // side + index
+            turn = (-index * side) % (2 * vectors)
+            value = jnp.where(
+                lane < vectors,
+                pltpu.roll(real, turn, 1) if turn else real,
+                pltpu.roll(imag, (turn + vectors) % (2 * vectors), 1)
+                if (turn + vectors) % (2 * vectors)
+                else imag,
+            )
+            value = jnp.where(own_half, -value, crossed[first * side : (first + 1) * side, :])
+            pair = first * vectors - first * (first + 1) // 2 + side - first - 1
+            ordered[pair : pair + side, :] = value
+    for first in range(vectors):
+        skip = first % side + 1
+        if skip < side:
+            pair = first * vectors - first * (first + 1) // 2
+            ordered[pair : pair + side - skip, :] = grid[
+                first * side + skip : (first + 1) * side, :
+            ]
 
 
 def last_chunk_kernel(
     tiles, first_tile, factor, place_ref, slot_ref, link_ref, low_ref, *refs
 ):
     ins, before, keep, send, sums, scratch = (
-        refs[:6], refs[6], refs[7], refs[8], refs[9], refs[10:-1],
+        refs[:6], refs[6], refs[7], refs[8], refs[9], refs[10:-3],
     )
-    ordered = refs[-1]
-
-    def store(plane, value):
-        @pl.when(plane == 0)
-        def _():
-            sums[...] = before[...] + value
-
-        @pl.when(plane > 0)
-        def _():
-            sums[...] += value
+    grid, crossed, ordered = refs[-3:]
+    sums[...] = before[...]
+
+    def store(plane, rows, value):
+        sums[rows, :] += value
 
     chunk_sums(tiles, first_tile, link_ref, low_ref, *ins, *scratch, store)
-    vectors = ins[0].shape[1]
-    for number, (left, right) in enumerate(pair_tiles(vectors)):
-        for row in range(ROWS):
-            first = left * ROWS + row
-            skip = max(0, first + 1 - right * ROWS)
-            if skip >= ROWS:
-                continue
-            second = right * ROWS + skip
-            pair = first * vectors - first * (first + 1) // 2 + second - first - 1
-            at = (number * ROWS + row) * ROWS
-            ordered[pair : pair + ROWS - skip, :] = sums[at + skip : at + ROWS, :] * factor
+    arrange(sums, grid, crossed, ordered, factor)
     keep[...] = jnp.zeros_like(keep)
     send[...] = jnp.zeros_like(send)
     chips = keep.shape[0]
@@ -445,7 +490,11 @@
         out_specs=[VMEM] * 2,
         scratch_shapes=[pltpu.VMEM((pair_rows, 2 * vectors), jnp.float32)]
         + scratch
-        + [pltpu.VMEM((blocks, 2 * vectors), jnp.float32)],
+        + [
+            pltpu.VMEM((vectors * vectors // 2, 2 * vectors), jnp.float32),
+            pltpu.VMEM((vectors * vectors // 4, 2 * vectors), jnp.float32),
+            pltpu.VMEM((blocks, 2 * vectors), jnp.float32),
+        ],
         compiler_params=params(48),
         cost_estimate=cost(8e9, 6 * piece_bytes),
         name="last_pairs",

time: 88.1 us -> 77.3 us (0.88)
  Pallas kernels: 41.9 us -> 31 us
    pallas_call x1, Pallas kernels: 13.8 us -> 7.99 us  [on_device(): pl.pallas_call(functools.partial(first_chunk_kernel, tiles), out_shape=pa...]
    pallas_call x1, Pallas kernels: 16 us -> 11 us  [on_device(): pl.pallas_call(functools.partial(last_chunk_kernel, tiles, c * per_chunk,...]
  transfers between devices with their start and end apart: 17 -> 17, of which waited for: 4 -> 4; matrix products, arithmetic and copies ran while one was open for 0% -> 0% of each run, Pallas kernels for 27% -> 23%
where the time goes in v2:
time: 77.3 us; the launch traced here: 77.1 us
  starting transfers between devices  38.7 us (50%)
  Pallas kernels  31 us (40%)
  waiting for transfers between devices  5.63 us (7%)
  local copies, waits for them, and re-layouts  1.51 us (2%)
    ppermute x7, starting transfers between devices, on_device(): lax.ppermute(shares[away], 'brick', [(i, (i // 2 + away) % chips * 2 + i...  12.4 us
    ppermute x4, starting transfers between devices, exchange(): lax.ppermute(fields[chunks + c], 'brick', upward)  12.4 us
    pallas_call x1, Pallas kernels, on_device(): pl.pallas_call(functools.partial(last_chunk_kernel, tiles, c * per_chunk,...  11 us
    ppermute x4, starting transfers between devices, exchange(): upper = [lax.ppermute(fields[c], 'brick', downward) for c in range(chunks)]  9.88 us
    pallas_call x2, Pallas kernels, local_hops(): pl.pallas_call(functools.partial(local_kernel, tiles, per_chunk), out_sha...  8.81 us
    pallas_call x1, Pallas kernels, on_device(): pl.pallas_call(functools.partial(first_chunk_kernel, tiles), out_shape=pa...  7.99 us
    ppermute x7, waiting for transfers between devices, on_device(): lax.ppermute(shares[away], 'brick', [(i, (i // 2 + away) % chips * 2 + i...  4.07 us
    ppermute x1, starting transfers between devices, on_device(): received = lax.ppermute(send, 'brick', [(i, i ^ 1) for i in range(count)])  3.95 us
  transfers between devices with their start and end apart: 17, of which 4 were waited for; matrix products, arithmetic and copies ran while one was open for 0% of the time, Pallas kernels for 23%

profile of v2, /device:TPU:0, one launch (start us, length us, event | category | flops | bytes accessed | tf_op | source)
XLA Modules:
  0.0 77.1 jit_solution(1183511763455635100)
XLA Ops:
  0.0 0.0 copy-start
  0.0 1.4 %copy-done = f32[64,2,3,2,512]{4,3,2,1,0:T(2,128)S(1)} copy-done((f32[64,2,3,2,512]{4,3,2,1,0:T(2,128)S(1)}, f32[64,2,3,2,512]{4,3,2,1,0:T(2,128)}, u32[]{:S(2)}) %copy-start) | copy-done | bytes 1572888
  1.4 0.0 copy-start.1
  1.4 1.7 %split.1 = (f32[6,64,256]{2,1,0:T(8,128)}, f32[6,64,256]{2,1,0:T(8,128)}, f32[6,64,256]{2,1,0:T(8,128)}, f32[6,64,256]{2,1,0:T(8,128)}) custom-call(f32[3072,128]{1,0:T(8,128)S(1)} %bitcast.15), custom_call_target="tpu_custom_call" | custom-call | tf_op jit(solution)/shard_map/split/pallas_call | solution.py:423
  3.1 0.5 collective-permute-start.5
  3.5 5.0 %collective-permute-start.6 = (f32[6,64,256]{2,1,0:T(8,128)}, f32[6,64,256]{2,1,0:T(8,128)S(1)}, u32[]{:S(2)}, u32[]{:S(2)}) collective-permute-start(f32[6,64,256]{2,1,0:T(8,128)} %get-tuple-element.33.refs_0_.refs_4_), channel_id=1, source_target_pairs={{1,0},{2,1},{3,2},{4,3},{5,4},{6,5},{7,6},{8,7},{9,8},{10,9},{11,1... | collective-permute-start | bytes 1179656 | tf_op jit(solution)/shard_map/ppermute | solution.py:434
  8.5 0.0 copy-done.1
  8.6 0.1 collective-permute-start
  8.7 0.1 collective-permute-start.1
  8.7 4.4 %collective-permute-start.2 = (f32[6,64,256]{2,1,0:T(8,128)}, f32[6,64,256]{2,1,0:T(8,128)S(1)}, u32[]{:S(2)}, u32[]{:S(2)}) collective-permute-start(f32[6,64,256]{2,1,0:T(8,128)} %get-tuple-element.32.refs_1_.refs_4_), channel_id=1, source_target_pairs={{1,0},{2,1},{3,2},{4,3},{5,4},{6,5},{7,6},{8,7},{9,8},{10,9},{11,1... | collective-permute-start | bytes 1179656 | tf_op jit(solution)/shard_map/ppermute | solution.py:434
  13.1 5.1 %local.2 = (f32[6,64,256]{2,1,0:T(8,128)S(1)}, f32[6,64,256]{2,1,0:T(8,128)S(1)}, f32[6,64,256]{2,1,0:T(8,128)S(1)}, f32[6,64,256]{2,1,0:T(8,128)S(1)}) custom-call(f32[432,128]{1,0:T(8,128)S(1)} %bitcast.16, f32[6,64,256]{2,1,0:T(8,128)} %get-tuple-element.33.refs_0_.refs_4_, f32[6,64,256]{2,1,0:T(8,128)} %get-tuple-element.32.refs_1_.refs_4_, ...), custom_call_target="tpu_custom_call" | custom-call | flops 5000000000 | bytes 3145728 | tf_op jit(solution)/shard_map/local/pallas_call | solution.py:438
  18.2 0.1 pad_add_fusion.place_ref
  18.3 0.0 collective-permute-done
  18.4 0.0 collective-permute-done.5.lower
  18.4 0.0 collective-permute-done.6.upper
  18.4 0.4 edge.3
  18.8 4.0 %collective-permute-start.7 = (f32[6,64,256]{2,1,0:T(8,128)S(1)}, f32[6,64,256]{2,1,0:T(8,128)S(1)}, u32[]{:S(2)}, u32[]{:S(2)}) collective-permute-start(f32[6,64,256]{2,1,0:T(8,128)S(1)} %get-tuple-element.42.refs_2_), channel_id=1, source_target_pairs={{0,1},{1,2},{2,3},{3,4},{4,5},{5,6},{6,7},{7,8},{8,9},{9,10},{10,1... | collective-permute-start | bytes 1179656 | tf_op jit(solution)/shard_map/ppermute | solution.py:433
  22.9 0.5 collective-permute-start.8
  23.3 0.0 collective-permute-done.1.lower
  23.3 0.0 collective-permute-done.2.upper
  23.3 0.4 edge.2
  23.7 7.9 %collective-permute-start.3 = (f32[6,64,256]{2,1,0:T(8,128)S(1)}, f32[6,64,256]{2,1,0:T(8,128)S(1)}, u32[]{:S(2)}, u32[]{:S(2)}) collective-permute-start(f32[6,64,256]{2,1,0:T(8,128)S(1)} %get-tuple-element.37.refs_3_), channel_id=1, source_target_pairs={{0,1},{1,2},{2,3},{3,4},{4,5},{5,6},{6,7},{7,8},{8,9},{9,10},{10,1... | collective-permute-start | bytes 1179656 | tf_op jit(solution)/shard_map/ppermute | solution.py:433
  31.6 0.0 collective-permute-start.4
  31.6 3.7 %local.3 = (f32[6,64,256]{2,1,0:T(8,128)S(1)}, f32[6,64,256]{2,1,0:T(8,128)S(1)}, f32[6,64,256]{2,1,0:T(8,128)S(1)}, f32[6,64,256]{2,1,0:T(8,128)S(1)}) custom-call(f32[432,128]{1,0:T(8,128)S(1)} %bitcast.19, f32[6,64,256]{2,1,0:T(8,128)S(1)} %get-tuple-element.41.refs_0_, f32[6,64,256]{2,1,0:T(8,128)S(1)} %get-tuple-element.38.refs_1_, ...), custom_call_target="tpu_custom_call" | custom-call | flops 5000000000 | bytes 3145728 | tf_op jit(solution)/shard_map/local/pallas_call | solution.py:438
  35.3 0.0 collective-permute-done.7.refs_0_
  35.3 0.0 collective-permute-done.8.refs_1_
  35.3 0.0 copy-start.2
  35.4 8.0 %pairs.1.refs_6_ = f32[1280,128]{1,0:T(8,128)S(1)} custom-call(f32[432,128]{1,0:T(8,128)S(1)} %bitcast.20, f32[72,128]{1,0:T(8,128)S(1)} %reshape.17.low_ref, f32[6,64,256]{2,1,0:T(8,128)S(1)} %collective-permute-done.7.refs_0_, f32[6,64,256]{2,1,0:T(8,128)S(1)} %collective-permute-done.8.refs_1_, f32[6,64,256]{2,1,0:T(8,128)S(1)} %get-tuple-element.45.refs_2_, ...), custom_call_target="tpu_custom_call" | custom-call | flops 8000000000 | bytes 2359296 | tf_op jit(solution)/shard_map/pairs/pallas_call | solution.py:469
  43.3 0.0 collective-permute-done.3.refs_0_
  43.4 0.0 collective-permute-done.4.refs_1_
  43.4 0.0 copy-done.2
  43.4 11.0 %last_pairs.1 = (f32[8,4,32,128]{3,2,1,0:T(8,128)S(1)}, f32[8,4,32,128]{3,2,1,0:T(8,128)S(1)}) custom-call(s32[2]{0:T(128)S(1)} %pad_add_fusion.place_ref, s32[63]{0:T(128)S(1)} %copy-done.2, f32[432,128]{1,0:T(8,128)S(1)} %bitcast.21, f32[72,128]{1,0:T(8,128)S(1)} %reshape.17.low_ref, f32[6,64,256]{2,1,0:T(8,128)S(1)} %collective-permute-done.3.refs_0_, ...), custom_call_target="tpu_custom_call" | custom-call | flops 8000000000 | bytes 2359296 | tf_op jit(solution)/shard_map/last_pairs/pallas_call | solution.py:486
  54.4 4.0 %collective-permute-start.9 = (f32[8,4,32,128]{3,2,1,0:T(8,128)S(1)}, f32[8,4,32,128]{3,2,1,0:T(8,128)S(1)}, u32[]{:S(2)}, u32[]{:S(2)}) collective-permute-start(f32[8,4,32,128]{3,2,1,0:T(8,128)S(1)} %get-tuple-element.48), channel_id=1, source_target_pairs={{0,1},{1,0},{2,3},{3,2},{4,5},{5,4},{6,7},{7,6},{8,9},{9,8},{10,11... | collective-permute-start | bytes 1572872 | tf_op jit(solution)/shard_map/ppermute | solution.py:505
  58.4 1.5 %collective-permute-done.9.received = f32[8,4,32,128]{3,2,1,0:T(8,128)S(1)} collective-permute-done((f32[8,4,32,128]{3,2,1,0:T(8,128)S(1)}, f32[8,4,32,128]{3,2,1,0:T(8,128)S(1)}, u32[]{:S(2)}, u32[]{:S(2)}) %collective-permute-start.9) | collective-permute-done | bytes 524320 | tf_op jit(solution)/shard_map/ppermute | solution.py:505
  59.9 0.1 combine.1
  60.0 0.1 collective-permute-start.10
  60.1 4.3 %collective-permute-start.11 = (f32[4,32,128]{2,1,0:T(8,128)S(1)}, f32[4,32,128]{2,1,0:T(8,128)S(1)}, u32[]{:S(2)}, u32[]{:S(2)}) collective-permute-start(f32[4,32,128]{2,1,0:T(8,128)S(1)} %get-tuple-element.51), channel_id=1, source_target_pairs={{0,4},{1,5},{2,6},{3,7},{4,8},{5,9},{6,10},{7,11},{8,12},{9,13},{1... | collective-permute-start | bytes 196616 | tf_op jit(solution)/shard_map/ppermute | solution.py:516
  64.4 1.1 %collective-permute-start.12 = (f32[4,32,128]{2,1,0:T(8,128)S(1)}, f32[4,32,128]{2,1,0:T(8,128)S(1)}, u32[]{:S(2)}, u32[]{:S(2)}) collective-permute-start(f32[4,32,128]{2,1,0:T(8,128)S(1)} %get-tuple-element.52), channel_id=1, source_target_pairs={{0,6},{1,7},{2,8},{3,9},{4,10},{5,11},{6,12},{7,13},{8,14},{9,15},... | collective-permute-start | bytes 196616 | tf_op jit(solution)/shard_map/ppermute | solution.py:516
  65.5 1.5 %collective-permute-start.13 = (f32[4,32,128]{2,1,0:T(8,128)S(1)}, f32[4,32,128]{2,1,0:T(8,128)S(1)}, u32[]{:S(2)}, u32[]{:S(2)}) collective-permute-start(f32[4,32,128]{2,1,0:T(8,128)S(1)} %get-tuple-element.53), channel_id=1, source_target_pairs={{0,8},{1,9},{2,10},{3,11},{4,12},{5,13},{6,14},{7,15},{8,0},{9,1},... | collective-permute-start | bytes 196616 | tf_op jit(solution)/shard_map/ppermute | solution.py:516
  67.0 2.3 %collective-permute-start.14 = (f32[4,32,128]{2,1,0:T(8,128)S(1)}, f32[4,32,128]{2,1,0:T(8,128)S(1)}, u32[]{:S(2)}, u32[]{:S(2)}) collective-permute-start(f32[4,32,128]{2,1,0:T(8,128)S(1)} %get-tuple-element.54), channel_id=1, source_target_pairs={{0,10},{1,11},{2,12},{3,13},{4,14},{5,15},{6,0},{7,1},{8,2},{9,3},... | collective-permute-start | bytes 196616 | tf_op jit(solution)/shard_map/ppermute | solution.py:516
  69.3 0.0 collective-permute-done.10.refs_1_
  69.3 2.9 %collective-permute-start.15 = (f32[4,32,128]{2,1,0:T(8,128)S(1)}, f32[4,32,128]{2,1,0:T(8,128)S(1)}, u32[]{:S(2)}, u32[]{:S(2)}) collective-permute-start(f32[4,32,128]{2,1,0:T(8,128)S(1)} %get-tuple-element.55), channel_id=1, source_target_pairs={{0,12},{1,13},{2,14},{3,15},{4,0},{5,1},{6,2},{7,3},{8,4},{9,5},{1... | collective-permute-start | bytes 196616 | tf_op jit(solution)/shard_map/ppermute | solution.py:516
  72.2 0.0 collective-permute-done.11.refs_2_
  72.2 0.2 collective-permute-start.16
  72.4 1.2 %collective-permute-done.12.refs_3_ = f32[4,32,128]{2,1,0:T(8,128)S(1)} collective-permute-done((f32[4,32,128]{2,1,0:T(8,128)S(1)}, f32[4,32,128]{2,1,0:T(8,128)S(1)}, u32[]{:S(2)}, u32[]{:S(2)}) %collective-permute-start.12) | collective-permute-done | bytes 65568 | tf_op jit(solution)/shard_map/ppermute | solution.py:516
  73.6 0.0 collective-permute-done.13.refs_4_
  73.6 0.0 collective-permute-done.14.refs_5_
  73.6 2.0 %collective-permute-done.15.refs_6_ = f32[4,32,128]{2,1,0:T(8,128)S(1)} collective-permute-done((f32[4,32,128]{2,1,0:T(8,128)S(1)}, f32[4,32,128]{2,1,0:T(8,128)S(1)}, u32[]{:S(2)}, u32[]{:S(2)}) %collective-permute-start.15) | collective-permute-done | bytes 65568 | tf_op jit(solution)/shard_map/ppermute | solution.py:516
  75.7 0.8 collective-permute-done.16.refs_7_
  76.5 0.7 total.1
  (4 shorter events, 0.1 us)
Async XLA Ops:
  0.0 1.4 %copy-start = (f32[64,2,3,2,512]{4,3,2,1,0:T(2,128)S(1)}, f32[64,2,3,2,512]{4,3,2,1,0:T(2,128)}, u32[]{:S(2)}) copy-start(f32[64,2,3,2,512]{4,3,2,1,0:T(2,128)} %param.3) | copy-start | bytes 4718596
  1.4 7.1 %copy-start.1 = (f32[3,2,3,3,2,512]{5,4,3,2,1,0:T(2,128)S(1)}, f32[3,2,3,3,2,512]{5,4,3,2,1,0:T(2,128)}, u32[]{:S(2)}) copy-start(f32[3,2,3,3,2,512]{5,4,3,2,1,0:T(2,128)} %param.4) | copy-start | bytes 663556
  3.1 15.3 %collective-permute-start.5 = (f32[6,64,256]{2,1,0:T(8,128)}, f32[6,64,256]{2,1,0:T(8,128)S(1)}, u32[]{:S(2)}, u32[]{:S(2)}) collective-permute-start(f32[6,64,256]{2,1,0:T(8,128)} %get-tuple-element.34.refs_2_.refs_5_), channel_id=1, source_target_pairs={{0,1},{1,2},{2,3},{3,4},{4,5},{5,6},{6,7},{7,8},{8,9},{9,10},{10,1... | collective-permute-start | bytes 1179656 | tf_op jit(solution)/shard_map/ppermute | solution.py:433
  3.5 14.9 %collective-permute-start.6 = (f32[6,64,256]{2,1,0:T(8,128)}, f32[6,64,256]{2,1,0:T(8,128)S(1)}, u32[]{:S(2)}, u32[]{:S(2)}) collective-permute-start(f32[6,64,256]{2,1,0:T(8,128)} %get-tuple-element.33.refs_0_.refs_4_), channel_id=1, source_target_pairs={{1,0},{2,1},{3,2},{4,3},{5,4},{6,5},{7,6},{8,7},{9,8},{10,9},{11,1... | collective-permute-start | bytes 1179656 | tf_op jit(solution)/shard_map/ppermute | solution.py:434
  8.6 9.7 %collective-permute-start = (f32[2,3,3,512]{3,0,2,1:T(2,128)S(1)}, f32[2,3,3,512]{3,0,2,1:T(2,128)S(1)}, u32[]{:S(2)}, u32[]{:S(2)}) collective-permute-start(f32[2,3,3,512]{3,0,2,1:T(2,128)S(1)} %bitcast.22), channel_id=1, source_target_pairs={{0,1},{1,2},{2,3},{3,4},{4,5},{5,6},{6,7},{7,8},{8,9},{9,10},{10,1... | collective-permute-start | bytes 110600 | tf_op jit(solution)/shard_map/ppermute | solution.py:420
  8.7 14.7 %collective-permute-start.1 = (f32[6,64,256]{2,1,0:T(8,128)}, f32[6,64,256]{2,1,0:T(8,128)S(1)}, u32[]{:S(2)}, u32[]{:S(2)}) collective-permute-start(f32[6,64,256]{2,1,0:T(8,128)} %get-tuple-element.31.refs_3_.refs_5_), channel_id=1, source_target_pairs={{0,1},{1,2},{2,3},{3,4},{4,5},{5,6},{6,7},{7,8},{8,9},{9,10},{10,1... | collective-permute-start | bytes 1179656 | tf_op jit(solution)/shard_map/ppermute | solution.py:433
  8.7 14.6 %collective-permute-start.2 = (f32[6,64,256]{2,1,0:T(8,128)}, f32[6,64,256]{2,1,0:T(8,128)S(1)}, u32[]{:S(2)}, u32[]{:S(2)}) collective-permute-start(f32[6,64,256]{2,1,0:T(8,128)} %get-tuple-element.32.refs_1_.refs_4_), channel_id=1, source_target_pairs={{1,0},{2,1},{3,2},{4,3},{5,4},{6,5},{7,6},{8,7},{9,8},{10,9},{11,1... | collective-permute-start | bytes 1179656 | tf_op jit(solution)/shard_map/ppermute | solution.py:434
  18.8 16.5 %collective-permute-start.7 = (f32[6,64,256]{2,1,0:T(8,128)S(1)}, f32[6,64,256]{2,1,0:T(8,128)S(1)}, u32[]{:S(2)}, u32[]{:S(2)}) collective-permute-start(f32[6,64,256]{2,1,0:T(8,128)S(1)} %get-tuple-element.42.refs_2_), channel_id=1, source_target_pairs={{0,1},{1,2},{2,3},{3,4},{4,5},{5,6},{6,7},{7,8},{8,9},{9,10},{10,1... | collective-permute-start | bytes 1179656 | tf_op jit(solution)/shard_map/ppermute | solution.py:433
  22.9 12.5 %collective-permute-start.8 = (f32[6,64,256]{2,1,0:T(8,128)S(1)}, f32[6,64,256]{2,1,0:T(8,128)S(1)}, u32[]{:S(2)}, u32[]{:S(2)}) collective-permute-start(f32[6,64,256]{2,1,0:T(8,128)S(1)} %get-tuple-element.41.refs_0_), channel_id=1, source_target_pairs={{1,0},{2,1},{3,2},{4,3},{5,4},{6,5},{7,6},{8,7},{9,8},{10,9},{11,1... | collective-permute-start | bytes 1179656 | tf_op jit(solution)/shard_map/ppermute | solution.py:434
  23.7 19.6 %collective-permute-start.3 = (f32[6,64,256]{2,1,0:T(8,128)S(1)}, f32[6,64,256]{2,1,0:T(8,128)S(1)}, u32[]{:S(2)}, u32[]{:S(2)}) collective-permute-start(f32[6,64,256]{2,1,0:T(8,128)S(1)} %get-tuple-element.37.refs_3_), channel_id=1, source_target_pairs={{0,1},{1,2},{2,3},{3,4},{4,5},{5,6},{6,7},{7,8},{8,9},{9,10},{10,1... | collective-permute-start | bytes 1179656 | tf_op jit(solution)/shard_map/ppermute | solution.py:433
  31.6 11.8 %collective-permute-start.4 = (f32[6,64,256]{2,1,0:T(8,128)S(1)}, f32[6,64,256]{2,1,0:T(8,128)S(1)}, u32[]{:S(2)}, u32[]{:S(2)}) collective-permute-start(f32[6,64,256]{2,1,0:T(8,128)S(1)} %get-tuple-element.38.refs_1_), channel_id=1, source_target_pairs={{1,0},{2,1},{3,2},{4,3},{5,4},{6,5},{7,6},{8,7},{9,8},{10,9},{11,1... | collective-permute-start | bytes 1179656 | tf_op jit(solution)/shard_map/ppermute | solution.py:434
  35.3 8.0 %copy-start.2 = (s32[63]{0:T(128)S(1)}, s32[63]{0:T(128)}, u32[]{:S(2)}) copy-start(s32[63]{0:T(128)} %slot_ref.1) | copy-start | bytes 760
  54.4 5.5 %collective-permute-start.9 = (f32[8,4,32,128]{3,2,1,0:T(8,128)S(1)}, f32[8,4,32,128]{3,2,1,0:T(8,128)S(1)}, u32[]{:S(2)}, u32[]{:S(2)}) collective-permute-start(f32[8,4,32,128]{3,2,1,0:T(8,128)S(1)} %get-tuple-element.48), channel_id=1, source_target_pairs={{0,1},{1,0},{2,3},{3,2},{4,5},{5,4},{6,7},{7,6},{8,9},{9,8},{10,11... | collective-permute-start | bytes 1572872 | tf_op jit(solution)/shard_map/ppermute | solution.py:505
  60.0 9.3 %collective-permute-start.10 = (f32[4,32,128]{2,1,0:T(8,128)S(1)}, f32[4,32,128]{2,1,0:T(8,128)S(1)}, u32[]{:S(2)}, u32[]{:S(2)}) collective-permute-start(f32[4,32,128]{2,1,0:T(8,128)S(1)} %get-tuple-element.50), channel_id=1, source_target_pairs={{0,2},{1,3},{2,4},{3,5},{4,6},{5,7},{6,8},{7,9},{8,10},{9,11},{10,... | collective-permute-start | bytes 196616 | tf_op jit(solution)/shard_map/ppermute | solution.py:516
  60.1 12.1 %collective-permute-start.11 = (f32[4,32,128]{2,1,0:T(8,128)S(1)}, f32[4,32,128]{2,1,0:T(8,128)S(1)}, u32[]{:S(2)}, u32[]{:S(2)}) collective-permute-start(f32[4,32,128]{2,1,0:T(8,128)S(1)} %get-tuple-element.51), channel_id=1, source_target_pairs={{0,4},{1,5},{2,6},{3,7},{4,8},{5,9},{6,10},{7,11},{8,12},{9,13},{1... | collective-permute-start | bytes 196616 | tf_op jit(solution)/shard_map/ppermute | solution.py:516
  64.4 9.2 %collective-permute-start.12 = (f32[4,32,128]{2,1,0:T(8,128)S(1)}, f32[4,32,128]{2,1,0:T(8,128)S(1)}, u32[]{:S(2)}, u32[]{:S(2)}) collective-permute-start(f32[4,32,128]{2,1,0:T(8,128)S(1)} %get-tuple-element.52), channel_id=1, source_target_pairs={{0,6},{1,7},{2,8},{3,9},{4,10},{5,11},{6,12},{7,13},{8,14},{9,15},... | collective-permute-start | bytes 196616 | tf_op jit(solution)/shard_map/ppermute | solution.py:516
  65.5 8.1 %collective-permute-start.13 = (f32[4,32,128]{2,1,0:T(8,128)S(1)}, f32[4,32,128]{2,1,0:T(8,128)S(1)}, u32[]{:S(2)}, u32[]{:S(2)}) collective-permute-start(f32[4,32,128]{2,1,0:T(8,128)S(1)} %get-tuple-element.53), channel_id=1, source_target_pairs={{0,8},{1,9},{2,10},{3,11},{4,12},{5,13},{6,14},{7,15},{8,0},{9,1},... | collective-permute-start | bytes 196616 | tf_op jit(solution)/shard_map/ppermute | solution.py:516
  67.0 6.7 %collective-permute-start.14 = (f32[4,32,128]{2,1,0:T(8,128)S(1)}, f32[4,32,128]{2,1,0:T(8,128)S(1)}, u32[]{:S(2)}, u32[]{:S(2)}) collective-permute-start(f32[4,32,128]{2,1,0:T(8,128)S(1)} %get-tuple-element.54), channel_id=1, source_target_pairs={{0,10},{1,11},{2,12},{3,13},{4,14},{5,15},{6,0},{7,1},{8,2},{9,3},... | collective-permute-start | bytes 196616 | tf_op jit(solution)/shard_map/ppermute | solution.py:516
  69.3 6.4 %collective-permute-start.15 = (f32[4,32,128]{2,1,0:T(8,128)S(1)}, f32[4,32,128]{2,1,0:T(8,128)S(1)}, u32[]{:S(2)}, u32[]{:S(2)}) collective-permute-start(f32[4,32,128]{2,1,0:T(8,128)S(1)} %get-tuple-element.55), channel_id=1, source_target_pairs={{0,12},{1,13},{2,14},{3,15},{4,0},{5,1},{6,2},{7,3},{8,4},{9,5},{1... | collective-permute-start | bytes 196616 | tf_op jit(solution)/shard_map/ppermute | solution.py:516
  72.2 4.3 %collective-permute-start.16 = (f32[4,32,128]{2,1,0:T(8,128)S(1)}, f32[4,32,128]{2,1,0:T(8,128)S(1)}, u32[]{:S(2)}, u32[]{:S(2)}) collective-permute-start(f32[4,32,128]{2,1,0:T(8,128)S(1)} %get-tuple-element.56), channel_id=1, source_target_pairs={{0,14},{1,15},{2,0},{3,1},{4,2},{5,3},{6,4},{7,5},{8,6},{9,7},{10,... | collective-permute-start | bytes 196616 | tf_op jit(solution)/shard_map/ppermute | solution.py:516
